TPU v7x, 128 devices: a whole 4x4x4 slice. The times are simulated.
128 devices in a mesh: pat: 16 (over y, x), obj: 8 (over z, core).
Axes of the slice: x: 4, y: 4, z: 4, core: 2. Of those that a mesh axis runs over, the one named last changes fastest.
Arguments:
- object_field: float32 [2, 1024, 16384], P(None, None, 'obj'), may hold values from -4 to 4
- probe: float32 [2, 256, 256], replicated, may hold values from -6 to 6
- amplitude: float32 [1024, 256, 256], P(('pat', 'obj')), may hold values from 0.1 to 3
- tile_owner: int32 [1024, 1], P(('pat', 'obj')), may hold values from 0 to 7; in each aligned block of 8 rows (0 to 7, 8 to 15, ...) at most 2 rows name the same one
- row_start: int32 [1024], P(('pat', 'obj')), may hold values from 0 to 768, as said below
- col_start: int32 [1024], P(('pat', 'obj')), may hold values from 0 to 1792
Outputs:
- object_grad: float32 [2, 1024, 16384], P(None, 'pat', 'obj')
- probe_grad: float32 [2, 256, 256], replicated
Inputs may be any that keep to these rules, and one draw needn't show every extreme that they name: `tile_owner`: among the patterns of one device at most 2 name the same tile, and in some device some tile is named by exactly 2. `row_start`: every pattern held by the devices of index g along pat starts its window at row min(g * 64 + e, 768) for some e with 0 <= e < 64.
All inputs are finite; a program needn't handle non-finite values.
Results may differ from a plain program's by a relative error of at most 0.0001.
Values sent between devices are 32-bit elements; how exact they have to be, the bound alone decides.
A program may use at most 192 MiB of HBM per device.

v0:
```python
import math

import jax
import jax.numpy as jnp
from jax import lax
from jax.sharding import PartitionSpec as P

CAP = 2


soften = 0.25


def dft_tables(length):
    index = jnp.arange(length, dtype=jnp.int32)
    phase = index[:, None] * index[None, :] % length
    angle = phase.astype(jnp.float32) * (2.0 * math.pi / length)
    factor = 1.0 / math.sqrt(length)
    return (jnp.cos(angle) * factor, -jnp.sin(angle) * factor)


def both_sides(real_part, imag_part, table_re, table_im):
    high = lax.Precision.HIGHEST
    left_re = jnp.einsum("jk,skl->sjl", table_re, real_part, precision=high) - jnp.einsum(
        "jk,skl->sjl", table_im, imag_part, precision=high
    )
    left_im = jnp.einsum("jk,skl->sjl", table_re, imag_part, precision=high) + jnp.einsum(
        "jk,skl->sjl", table_im, real_part, precision=high
    )
    right_re = jnp.einsum("sjk,kl->sjl", left_re, table_re, precision=high) - jnp.einsum(
        "sjk,kl->sjl", left_im, table_im, precision=high
    )
    right_im = jnp.einsum("sjk,kl->sjl", left_re, table_im, precision=high) + jnp.einsum(
        "sjk,kl->sjl", left_im, table_re, precision=high
    )
    return (right_re, right_im)


def residual_waves(windows, patterns, wanted, probe):
    window_re = windows[:, 0]
    window_im = windows[:, 1]
    probe_re = probe[0]
    probe_im = probe[1]
    exit_re = probe_re * window_re - probe_im * window_im
    exit_im = probe_re * window_im + probe_im * window_re
    table_re, table_im = dft_tables(windows.shape[-1])
    spec_re, spec_im = both_sides(exit_re, exit_im, table_re, table_im)
    ratio = patterns / jnp.sqrt(spec_re * spec_re + spec_im * spec_im + soften)
    back_re, back_im = both_sides(spec_re * ratio, spec_im * ratio, table_re, -table_im)
    keeper = (wanted > 0).astype(jnp.float32)[:, None, None]
    return jnp.stack([(back_re - exit_re) * keeper, (back_im - exit_im) * keeper], axis=1)


def cut_windows(object_field, top_rows, left_cols, width):

    def cut_one(top_row, left_col):
        return lax.dynamic_slice(object_field, (jnp.int32(0), top_row, left_col), (2, width, width))

    return jax.vmap(cut_one)(top_rows, left_cols)


def on_device(object_field, probe, amplitude, tile_owner, row_start, col_start):
    owners = lax.axis_size("obj")
    groups = lax.axis_size("pat")
    width = amplitude.shape[-1]
    count = amplitude.shape[0]
    slots = owners * CAP

    def by_owner(values):
        return values.reshape((owners, CAP) + values.shape[1:])

    def by_slot(values):
        return values.reshape((slots,) + values.shape[2:])

    owner_ids = tile_owner[:, 0]
    owner_hot = (owner_ids[:, None] == jnp.arange(owners, dtype=jnp.int32)[None, :]).astype(
        jnp.int32
    )
    position = jnp.arange(count, dtype=jnp.int32)
    earlier = (position[:, None] > position[None, :]).astype(jnp.int32)
    ranking = jnp.sum(jnp.dot(earlier, owner_hot) * owner_hot, axis=1)
    slot_of = owner_ids * CAP + ranking
    slot_hot = slot_of[:, None] == jnp.arange(slots, dtype=jnp.int32)[None, :]
    wanted = jnp.sum(slot_hot.astype(jnp.int32), axis=0)
    want_rows = jnp.sum(jnp.where(slot_hot, row_start[:, None], 0), axis=0)
    want_cols = jnp.sum(jnp.where(slot_hot, col_start[:, None], 0), axis=0)
    slot_amps = jnp.einsum(
        "js,jpq->spq", slot_hot.astype(jnp.float32), amplitude, precision=lax.Precision.HIGHEST
    )
    got_rows, got_cols, got_wanted = (
        lax.all_to_all(by_owner(want_rows), "obj", split_axis=0, concat_axis=0, tiled=True),
        lax.all_to_all(by_owner(want_cols), "obj", split_axis=0, concat_axis=0, tiled=True),
        lax.all_to_all(by_owner(wanted), "obj", split_axis=0, concat_axis=0, tiled=True),
    )
    top_rows = by_slot(got_rows)
    left_cols = by_slot(got_cols)
    windows = cut_windows(object_field, top_rows, left_cols, width)
    arrived = lax.all_to_all(by_owner(windows), "obj", split_axis=0, concat_axis=0, tiled=True)
    local_res = residual_waves(by_slot(arrived), slot_amps, wanted, probe)
    residual = by_slot(
        lax.all_to_all(by_owner(local_res), "obj", split_axis=0, concat_axis=0, tiled=True)
    )
    probe_re = probe[0]
    probe_im = probe[1]
    res_re = residual[:, 0]
    res_im = residual[:, 1]
    window_re = windows[:, 0]
    window_im = windows[:, 1]
    update = jnp.stack(
        [probe_re * res_re + probe_im * res_im, probe_re * res_im - probe_im * res_re], axis=1
    )
    probe_part = jnp.stack(
        [
            jnp.sum(window_re * res_re + window_im * res_im, axis=0),
            jnp.sum(window_re * res_im - window_im * res_re, axis=0),
        ]
    )

    def add_window(number, gradient):
        corner = (jnp.int32(0), top_rows[number], left_cols[number])
        before = lax.dynamic_slice(gradient, corner, (2, width, width))
        return lax.dynamic_update_slice(gradient, before + update[number], corner)

    gradient = lax.fori_loop(0, slots, add_window, jnp.zeros(object_field.shape, jnp.float32))
    object_grad = lax.psum_scatter(gradient, "pat", scatter_dimension=1, tiled=True)
    probe_total = lax.psum(probe_part, ("pat", "obj"))
    patterns = count * groups * owners
    return (object_grad, probe_total / math.sqrt(patterns))


def solution(mesh):
    return jax.shard_map(
        on_device,
        mesh=mesh,
        in_specs=(
            P(None, None, "obj"),
            P(),
            P(("pat", "obj"), None, None),
            P(("pat", "obj"), None),
            P(("pat", "obj")),
            P(("pat", "obj")),
        ),
        out_specs=(P(None, "pat", "obj"), P()),
        check_vma=False,
    )
```

profile of v0, /device:TPU:1, one launch (start us, length us, event | category | flops | bytes accessed | tf_op | source)
XLA Modules:
  0.0 832.7 jit_solution(11390096830806761210)
XLA Ops:
  11.1 6.8 all-to-all-start
  18.5 3.8 all-to-all-done
  22.4 3.9 all-to-all-start.1
  26.4 4.4 all-to-all-done.1
  30.9 65.0 %while.15 = (s32[]{:T(128)}, f32[2,1024,2048]{2,1,0:T(8,128)}, s32[16,3]{0,1:T(4,128)S(1)}, f32[16,2,256,256]{3,2,1,0:T(8,128)}, s32[]{:T(128)}) while((s32[]{:T(128)}, f32[2,1024,2048]{2,1,0:T(8,128)}, s32[16,3]{0,1:T(4,128)S(1)}, f32[16,2,256,256]{3,2,1,0:T(8,128)}, s32[]{:T(128)}) %tuple.55), condition=%wide.while_cond, body=%wide.while_body.sunk | while | flops 2 | bytes 1049717 | solution.py:57
  35.6 3.5 bitcast_dynamic-update-slice_fusion.2
  39.6 3.5 bitcast_dynamic-update-slice_fusion.2
  43.7 3.5 bitcast_dynamic-update-slice_fusion.2
  47.8 3.5 bitcast_dynamic-update-slice_fusion.2
  51.8 3.5 bitcast_dynamic-update-slice_fusion.2
  59.9 3.5 bitcast_dynamic-update-slice_fusion.2
  64.0 3.5 bitcast_dynamic-update-slice_fusion.2
  68.0 3.5 bitcast_dynamic-update-slice_fusion.2
  72.1 3.5 bitcast_dynamic-update-slice_fusion.2
  76.2 3.5 bitcast_dynamic-update-slice_fusion.2
  80.2 3.5 bitcast_dynamic-update-slice_fusion.2
  84.3 3.5 bitcast_dynamic-update-slice_fusion.2
  92.4 3.5 bitcast_dynamic-update-slice_fusion.2
  95.9 7.5 copy.73
  103.4 5.7 all-to-all-start.2
  109.2 4.3 fusion.28
  113.4 89.5 %all-to-all-done.2 = f32[8,2,2,256,256]{4,3,1,2,0:T(8,128)} async-done(((f32[8,2,2,256,256]{4,3,1,2,0:T(8,128)}), f32[8,2,2,256,256]{4,3,1,2,0:T(8,128)}, u32[]{:S(2)}, u32[]{:S(2)}) %all-to-all-start.2) | async-done | bytes 8388640 | tf_op jit(solution)/shard_map/all_to_all | solution.py:98
  203.0 4.3 copy.74
  208.7 8.1 fusion.52
  216.8 8.5 %fusion.49 = f32[16,256,256]{2,1,0:T(8,128)S(1)} fusion(f32[16,256,256]{2,1,0:T(8,128)S(1)} %get-tuple-element.133), kind=kOutput, calls=%fused_computation.66 | convolution fusion | flops 3222208512 | bytes 8388608 | tf_op jit(solution)/shard_map/jk,skl->sjl/dot_general | solution.py:27
  225.3 8.3 %convolution_add_fusion.1 = f32[16,256,256]{2,1,0:T(8,128)S(1)} fusion(f32[16,256,256]{2,1,0:T(8,128)S(1)} %fusion.49, f32[16,256,256]{2,1,0:T(8,128)S(1)} %get-tuple-element.132), kind=kOutput, calls=%fused_computation.38 | convolution fusion | flops 3223322624 | bytes 12582912 | tf_op jit(solution)/shard_map/jk,skl->sjl/dot_general | solution.py:27
  233.7 8.2 fusion.8
  241.8 8.4 %fusion.10 = f32[16,256,256]{2,1,0:T(8,128)S(1)} fusion(f32[16,256,256]{2,1,0:T(8,128)S(1)} %convolution_add_fusion.1), kind=kOutput, calls=%fused_computation.17 | convolution fusion | flops 3222274048 | bytes 8388608 | tf_op jit(solution)/shard_map/sjk,kl->sjl/dot_general | solution.py:30
  250.2 8.2 convolution_subtract_fusion.1
  258.4 8.5 %fusion.21 = f32[16,256,256]{2,1,0:T(8,128)S(1)} fusion(f32[16,256,256]{2,1,0:T(8,128)S(1)} %fusion.8, f32[16,256,256]{2,1,0:T(8,128)S(1)} %convolution_subtract_fusion.1), kind=kOutput, calls=%fused_computation.35 | convolution fusion | flops 3223322624 | bytes 12582912 | tf_op jit(solution)/shard_map/sjk,kl->sjl/dot_general | solution.py:33
  266.9 8.5 %fusion.18 = f32[16,256,256]{2,1,0:T(8,128)S(1)} fusion(f32[16,256,256]{2,1,0:T(8,128)S(1)} %fusion.10, f32[16,256,256]{2,1,0:T(8,128)S(1)} %convolution_subtract_fusion.1), kind=kOutput, calls=%fused_computation.34 | convolution fusion | flops 3223257088 | bytes 12582912 | tf_op jit(solution)/shard_map/sjk,kl->sjl/dot_general | solution.py:30
  275.4 12.0 %fusion.43 = f32[16,256,256]{2,1,0:T(8,128)} fusion(f32[16,256,256]{2,1,0:T(8,128)S(1)} %fusion.21, f32[16,256,256]{2,0,1:T(8,128)S(1)} %copy-done.2, f32[16,256,256]{2,1,0:T(8,128)S(1)} %fusion.18), kind=kOutput, calls=%fused_computation.60 | convolution fusion | flops 3228499968 | bytes 16777216 | tf_op jit(solution)/shard_map/jk,skl->sjl/dot_general | solution.py:27
  287.4 12.6 %convolution_add_fusion = f32[16,256,256]{2,1,0:T(8,128)S(1)} fusion(f32[16,256,256]{2,1,0:T(8,128)} %fusion.43, f32[16,256,256]{2,1,0:T(8,128)S(1)} %fusion.18, f32[16,256,256]{2,0,1:T(8,128)S(1)} %copy-done.2, f32[16,256,256]{2,1,0:T(8,128)S(1)} %fusion.21), kind=kOutput, calls=%fused_computation.36 | convolution fusion | flops 3229679616 | bytes 20971520 | tf_op jit(solution)/shard_map/jk,skl->sjl/dot_general | solution.py:27
  300.1 10.8 %fusion = f32[16,256,256]{2,1,0:T(8,128)} fusion(f32[16,256,256]{2,1,0:T(8,128)S(1)} %convolution_add_fusion), kind=kOutput, calls=%fused_computation.7 | convolution fusion | flops 3222208512 | bytes 8388608 | tf_op jit(solution)/shard_map/sjk,kl->sjl/dot_general | solution.py:33
  310.8 10.5 %fusion.2 = f32[16,256,256]{2,1,0:T(8,128)} fusion(f32[16,256,256]{2,1,0:T(8,128)S(1)} %convolution_add_fusion), kind=kOutput, calls=%fused_computation.9 | convolution fusion | flops 3222339584 | bytes 8388608 | tf_op jit(solution)/shard_map/sjk,kl->sjl/dot_general | solution.py:30
  321.4 11.8 %fusion.46 = f32[16,256,256]{2,1,0:T(8,128)} fusion(f32[16,256,256]{2,1,0:T(8,128)S(1)} %fusion.18, f32[16,256,256]{2,0,1:T(8,128)S(1)} %copy-done.2, f32[16,256,256]{2,1,0:T(8,128)S(1)} %fusion.21), kind=kOutput, calls=%fused_computation.63 | convolution fusion | flops 3228499968 | bytes 16777216 | tf_op jit(solution)/shard_map/jk,skl->sjl/dot_general | solution.py:24
  333.2 12.8 %convolution_subtract_fusion = f32[16,256,256]{2,1,0:T(8,128)S(1)} fusion(f32[16,256,256]{2,1,0:T(8,128)} %fusion.46, f32[16,256,256]{2,1,0:T(8,128)S(1)} %fusion.21, f32[16,256,256]{2,0,1:T(8,128)S(1)} %copy-done.2, f32[16,256,256]{2,1,0:T(8,128)S(1)} %fusion.18), kind=kOutput, calls=%fused_computation.37 | convolution fusion | flops 3229679616 | bytes 20971520 | tf_op jit(solution)/shard_map/jk,skl->sjl/dot_general | solution.py:24
  346.0 13.2 %subtract_multiply_fusion = f32[16,256,256]{2,1,0:T(8,128)} fusion(f32[16,256,256]{2,1,0:T(8,128)S(1)} %get-tuple-element.133, f32[16,256,256]{2,1,0:T(8,128)} %fusion, f32[16,256,256]{2,1,0:T(8,128)S(1)} %convolution_subtract_fusion, f32[16]{0:T(128)S(1)} %compare_convert_fusion), kind=kOutput, calls=%fused_computation.28 | convolution fusion | flops 3225485312 | bytes 16777280 | tf_op jit(solution)/shard_map/sjk,kl->sjl/dot_general | solution.py:33
  359.2 11.1 %subtract_multiply_fusion.1 = f32[16,256,256]{2,1,0:T(8,128)} fusion(f32[16,256,256]{2,1,0:T(8,128)S(1)} %get-tuple-element.132, f32[16,256,256]{2,1,0:T(8,128)S(1)} %copy-done.3, f32[16,256,256]{2,1,0:T(8,128)S(1)} %convolution_subtract_fusion, f32[16]{0:T(128)S(1)} %compare_convert_fusion), kind=kOutput, calls=%fused_computation.29 | convolution fusion | flops 3225354240 | bytes 16777280 | tf_op jit(solution)/shard_map/sjk,kl->sjl/dot_general | solution.py:30
  370.3 6.3 pad_maximum_fusion
  376.6 5.7 all-to-all-start.3
  384.3 91.9 %all-to-all-done.3 = f32[8,2,2,256,256]{4,3,1,2,0:T(8,128)} async-done(((f32[8,2,2,256,256]{4,3,1,2,0:T(8,128)}), f32[8,2,2,256,256]{4,3,1,2,0:T(8,128)}, u32[]{:S(2)}, u32[]{:S(2)}) %all-to-all-start.3) | async-done | bytes 8388640 | tf_op jit(solution)/shard_map/all_to_all | solution.py:101
  476.2 3.9 copy.95
  480.1 6.8 add_reduce_fusion
  487.8 7.6 pad_maximum_fusion.1
  495.4 7.8 broadcast_in_dim.20
  503.2 206.7 %while.14 = (s32[]{:T(128)}, f32[2,1024,2048]{2,1,0:T(8,128)}, s32[16]{0:T(128)S(1)}, s32[16]{0:T(128)S(1)}, f32[16,2,256,256]{3,2,1,0:T(8,128)}, /*index=5*/s32[]{:T(128)}, s32[]{:T(128)}, s32[]{:T(128)}, s32[]{:T(128)}) while((s32[]{:T(128)}, f32[2,1024,2048]{2,1,0:T(8,128)}, s32[16]{0:T(128)S(1)}, s32[16]{0:T(128)S(1)}, ...), condition=%wide.region_5.6_spmd, body=%wide.region_4.5_spmd.sunk | while | flops 131080 | bytes 2621649 | solution.py:124
  509.8 6.8 dynamic_update_slice.8
  523.2 6.0 dynamic_update_slice.8
  535.8 6.5 dynamic_update_slice.8
  548.9 6.0 dynamic_update_slice.8
  561.5 6.8 dynamic_update_slice.8
  574.9 6.0 dynamic_update_slice.8
  587.4 6.8 dynamic_update_slice.8
  600.8 6.0 dynamic_update_slice.8
  613.3 6.8 dynamic_update_slice.8
  626.7 6.0 dynamic_update_slice.8
  639.3 6.5 dynamic_update_slice.8
  652.4 6.0 dynamic_update_slice.8
  664.9 6.8 dynamic_update_slice.8
  678.3 6.0 dynamic_update_slice.8
  690.9 6.5 dynamic_update_slice.8
  704.0 6.0 dynamic_update_slice.8
  712.0 112.8 %reduce-scatter.2.cloned.1.call-done = f32[2,64,2048]{2,1,0:T(8,128)} async-done(((f32[2,1024,2048]{2,1,0:T(8,128)}), f32[2,64,2048]{2,1,0:T(8,128)}) %reduce-scatter.2.cloned.1.call-update) | async-done | bytes 1048592 | tf_op jit(solution)/shard_map/reduce_scatter | solution.py:125
  (121 shorter events, 75.0 us)
Async XLA Ops:
  8.0 101.2 %copy-start = (f32[8,256,256]{2,1,0:T(8,128)S(1)}, f32[8,256,256]{2,1,0:T(8,128)}, u32[]{:S(2)}) copy-start(f32[8,256,256]{2,1,0:T(8,128)} %param.10) | copy-start | bytes 6291460
  11.1 11.3 %all-to-all-start = ((s32[8,1,2]{2,1,0:T(1,128)}), s32[8,1,2]{2,1,0:T(1,128)S(1)}, u32[]{:S(2)}, u32[]{:S(2)}) async-start(s32[8,1,2]{2,1,0:T(1,128)} %bitcast.6), calls=%async_computation | async-start | bytes 8192 | tf_op jit(solution)/shard_map/all_to_all | solution.py:91
  22.4 8.4 %all-to-all-start.1 = ((s32[8,1,2]{2,1,0:T(1,128)}), s32[8,1,2]{2,1,0:T(1,128)S(1)}, u32[]{:S(2)}, u32[]{:S(2)}) async-start(s32[8,1,2]{2,1,0:T(1,128)} %bitcast.7), calls=%async_computation.1 | async-start | bytes 8192 | tf_op jit(solution)/shard_map/all_to_all | solution.py:92
  103.4 5.7 copy-start.5
  103.4 99.6 %all-to-all-start.2 = ((f32[8,2,2,256,256]{4,3,1,2,0:T(8,128)}), f32[8,2,2,256,256]{4,3,1,2,0:T(8,128)}, u32[]{:S(2)}, u32[]{:S(2)}) async-start(f32[8,2,2,256,256]{4,3,1,2,0:T(8,128)} %copy.73), calls=%async_computation.2 | async-start | bytes 16777216 | tf_op jit(solution)/shard_map/all_to_all | solution.py:98
  266.9 8.5 %copy-start.2 = (f32[16,256,256]{2,0,1:T(8,128)S(1)}, f32[16,256,256]{2,0,1:T(8,128)}, u32[]{:S(2)}) copy-start(f32[16,256,256]{2,0,1:T(8,128)} %fusion.28) | copy-start | bytes 12582916
  346.0 13.2 %copy-start.3 = (f32[16,256,256]{2,1,0:T(8,128)S(1)}, f32[16,256,256]{2,1,0:T(8,128)}, u32[]{:S(2)}) copy-start(f32[16,256,256]{2,1,0:T(8,128)} %fusion.2) | copy-start | bytes 12582916
  359.2 11.1 %copy-start.4 = (f32[16,256,256]{2,1,0:T(8,128)S(1)}, f32[16,256,256]{2,1,0:T(8,128)}, u32[]{:S(2)}) copy-start(f32[16,256,256]{2,1,0:T(8,128)} %subtract_multiply_fusion) | copy-start | bytes 12582916
  376.6 99.6 %all-to-all-start.3 = ((f32[8,2,2,256,256]{4,3,1,2,0:T(8,128)}), f32[8,2,2,256,256]{4,3,1,2,0:T(8,128)}, u32[]{:S(2)}, u32[]{:S(2)}) async-start(f32[8,2,2,256,256]{4,3,1,2,0:T(8,128)} %pad_maximum_fusion), calls=%async_computation.3 | async-start | bytes 16777216 | tf_op jit(solution)/shard_map/all_to_all | solution.py:101
  382.3 327.7 %all-reduce.2.cloned.1.call-start = ((), (), s32[]{:S(2)}) async-start(), calls=%async_computation.6 | async-start | bytes 1048576 | tf_op jit(solution)/shard_map/psum | solution.py:126
  487.8 337.0 %reduce-scatter.2.cloned.1.call-start = ((), (), s32[]{:S(2)}) async-start(), calls=%async_computation.5 | async-start | bytes 17825792 | tf_op jit(solution)/shard_map/reduce_scatter | solution.py:125
  710.0 114.8 %copy-start.1 = (f32[8,256,256]{2,1,0:T(8,128)S(1)}, f32[8,256,256]{2,1,0:T(8,128)}, u32[]{:S(2)}) copy-start(f32[8,256,256]{2,1,0:T(8,128)} %param.10) | copy-start | bytes 6291460
Sparse Core Ops, SparseCore 0:
  487.9 144.9 all-reduce.1
Sparse Core Ops, SparseCore 1:
  710.0 114.7 reduce-scatter.1
where the time goes:
time: 842 us; the launch traced here: 833 us
  waiting for transfers between devices  302 us (36%)
  local copies, waits for them, and re-layouts  212 us (25%)
  matrix products  167 us (20%)
  loops' own time  60.7 us (7%)
  other arithmetic  52.1 us (6%)
  starting transfers between devices  22.2 us (3%)
  between operations  16.2 us (2%)
    reduce_scatter x1, waiting for transfers between devices, on_device(): lax.psum_scatter(gradient, 'pat', scatter_dimension=1, tiled=True)  113 us
    dynamic_update_slice x16, local copies, waits for them, and re-layouts, add_window(): return lax.dynamic_update_slice(gradient, before + update[number], corner)  101 us
    all_to_all x1, waiting for transfers between devices, on_device(): lax.all_to_all(by_owner(local_res), 'obj', split_axis=0, concat_axis=0, t...  91.9 us
    all_to_all x1, waiting for transfers between devices, on_device(): lax.all_to_all(by_owner(windows), 'obj', split_axis=0, concat_axis=0, til...  89.5 us
    gather x48, local copies, waits for them, and re-layouts  64.9 us
    another operation x1, loops' own time, on_device(): lax.fori_loop(0, slots, add_window, jnp.zeros(object_field.shape, jnp.flo...  60.6 us
    add x16, other arithmetic, add_window(): return lax.dynamic_update_slice(gradient, before + update[number], corner)  24.5 us
    dot_general x2, matrix products, both_sides(): jnp.einsum('sjk,kl->sjl', left_re, table_im, precision=high)  21.8 us
  transfers between devices with their start and end apart: 6, of which 5 were waited for; matrix products, arithmetic and copies ran while one was open for 20% of the time, Pallas kernels for 0%

commit v1 on v0

v1 whole, which is shorter than its diff:
```python
import math

import jax
import jax.numpy as jnp
import numpy as np
from jax import lax
from jax.experimental import pallas as pl
from jax.experimental.pallas import tpu as pltpu
from jax.sharding import PartitionSpec as P

MESH = pl.DeviceIdType.MESH
CAP = 2
SIDE = 256
HALF = 128
STRIP = 64
SPAN = 320
TILE = 2048
BLOCKS = TILE // HALF
SOFTEN = 0.25
OWNERS = 8
COUNT = 8
SLOTS = OWNERS * CAP
NX = 4
NY = 4
CHUNKS = 8
CHUNK = BLOCKS // CHUNKS
F32 = jnp.float32
BF16 = jnp.bfloat16
ANY = pl.BlockSpec(memory_space=pl.ANY)
VMEM = pl.BlockSpec(memory_space=pltpu.VMEM)
SMEM = pl.BlockSpec(memory_space=pltpu.SMEM)


def dft_tables():
    index = np.arange(SIDE)
    full = np.exp(-2j * np.pi * (np.outer(index, index) % SIDE) / SIDE) / math.sqrt(SIDE)

    def right(table):
        return np.block([[table.real, table.imag], [-table.imag, table.real]])

    swap = np.roll(np.arange(HALF), -HALF // 2)
    half = [full[:HALF, 0::2], full[:HALF, 1::2]]
    lane = [half[0], half[1][:, swap]]
    tables = [
        right(lane[0]),
        right(lane[1]),
        right(half[0]).T,
        right(half[1]).T,
        right(half[0].conj().T).T,
        right(half[1].conj().T).T,
        right(lane[0].conj().T),
        right(lane[1].conj().T),
    ]
    exact = np.stack(tables).astype(np.float32)
    high = exact.astype(BF16)
    low = (exact - high.astype(np.float32)).astype(BF16)
    return np.stack([high, low], axis=1)


def split(value):
    high = value.astype(BF16)
    return high, (value - high.astype(F32)).astype(BF16)


def times_table(data, table):
    high, low = split(data)
    left = jnp.concatenate([high, low, high], axis=1)
    right = jnp.concatenate([table[0], table[0], table[1]], axis=0)
    return jnp.dot(left, right, preferred_element_type=F32)


def table_times(table, data):
    high, low = split(data)
    left = jnp.concatenate([table[0], table[0], table[1]], axis=1)
    right = jnp.concatenate([high, low, high], axis=0)
    return jnp.dot(left, right, preferred_element_type=F32)


def beside(*parts):
    return jnp.concatenate(parts, axis=1)


def above(*parts):
    return jnp.concatenate(parts, axis=0)


def by_parity(rows):
    lane = lax.broadcasted_iota(jnp.int32, (HALF, HALF), 1)
    front = lane < HALF // 2
    first = jnp.take_along_axis(
        rows[:, :HALF], jnp.where(front, 2 * lane, 2 * lane - HALF + 1), axis=1, mode="promise_in_bounds"
    )
    second = jnp.take_along_axis(
        rows[:, HALF:], jnp.where(front, 2 * lane + 1, 2 * lane - HALF), axis=1, mode="promise_in_bounds"
    )
    return beside(jnp.where(front, first, second), jnp.where(front, second, first))


def residual_wave(exit_re, exit_im, wanted_rows, tables):
    front = slice(0, HALF)
    back = slice(HALF, SIDE)
    even = times_table(
        beside(exit_re[:, front] + exit_re[:, back], exit_im[:, front] + exit_im[:, back]), tables(0)
    )
    odd = times_table(
        beside(exit_re[:, front] - exit_re[:, back], exit_im[:, front] - exit_im[:, back]), tables(1)
    )
    re = beside(even[:, front], odd[:, front])
    im = beside(even[:, back], odd[:, back])
    spectrum = [
        table_times(tables(2), above(re[front] + re[back], im[front] + im[back])),
        table_times(tables(3), above(re[front] - re[back], im[front] - im[back])),
    ]
    scaled = []
    for parity in range(2):
        re, im = spectrum[parity][front], spectrum[parity][back]
        ratio = wanted_rows(parity) * lax.rsqrt(re * re + im * im + SOFTEN)
        scaled.append(above(re * ratio, im * ratio))
    even = table_times(tables(4), scaled[0])
    odd = table_times(tables(5), scaled[1])
    re = above(even[front] + odd[front], even[front] - odd[front])
    im = above(even[back] + odd[back], even[back] - odd[back])
    even = times_table(beside(re[:, front], im[:, front]), tables(6))
    odd = times_table(beside(re[:, back], im[:, back]), tables(7))
    back_re = beside(even[:, front] + odd[:, front], even[:, front] - odd[:, front])
    back_im = beside(even[:, back] + odd[:, back], even[:, back] - odd[:, back])
    return back_re - exit_re, back_im - exit_im


def pack_kernel(owner_ref, row_ref, col_ref, amp_ref, packed_ref, meta_ref, sems):
    ranks = []
    copies = []
    for j in range(COUNT):
        rank = jnp.int32(0)
        for i in range(j):
            rank = rank + (owner_ref[i, 0] == owner_ref[j, 0]).astype(jnp.int32)
        ranks.append(rank)
        for side in range(2):
            copy = pltpu.make_async_copy(
                amp_ref.at[j, :, pl.ds(side * HALF, HALF)],
                packed_ref.at[owner_ref[j, 0], rank, side],
                sems.at[j, side],
            )
            copy.start()
            copies.append(copy)
    meta_ref[...] = jnp.zeros_like(meta_ref)
    sub = lax.broadcasted_iota(jnp.int32, (8, 128), 0)
    for j in range(COUNT):
        shape = (sub // 4 == ranks[j]) & (sub % 4 < 3)
        value = jnp.where(
            sub % 4 == 0, 1, jnp.where(sub % 4 == 1, row_ref[j], col_ref[j])
        )
        tile = meta_ref[owner_ref[j, 0]]
        meta_ref[owner_ref[j, 0]] = jnp.where(shape, value, tile)
    for copy in copies:
        copy.wait()


def pack(tile_owner, row_start, col_start, amplitude):
    return pl.pallas_call(
        pack_kernel,
        out_shape=(
            jax.ShapeDtypeStruct((OWNERS, CAP, 2, SIDE, HALF), F32),
            jax.ShapeDtypeStruct((OWNERS, 8, 128), jnp.int32),
        ),
        in_specs=[SMEM, SMEM, SMEM, ANY],
        out_specs=(ANY, VMEM),
        scratch_shapes=[pltpu.SemaphoreType.DMA((COUNT, 2))],
        name="pack",
    )(tile_owner, row_start, col_start, amplitude)


def exchange_kernel(packed_ref, meta_ref, got_ref, got_meta_ref, here, send, recv, send_meta, recv_meta):
    me = lax.axis_index("obj")
    barrier = pltpu.get_barrier_semaphore()
    for k in range(1, OWNERS):
        pl.semaphore_signal(
            barrier, inc=1, device_id={"obj": lax.rem(me + k, OWNERS)}, device_id_type=MESH
        )
    pl.semaphore_wait(barrier, OWNERS - 1)
    copies = []
    for k in range(1, OWNERS):
        there = lax.rem(me + k, OWNERS)
        copies.append(
            pltpu.make_async_remote_copy(
                src_ref=meta_ref.at[there],
                dst_ref=got_meta_ref.at[me],
                send_sem=send_meta.at[k],
                recv_sem=recv_meta.at[k],
                device_id={"obj": there},
                device_id_type=MESH,
            )
        )
        copies.append(
            pltpu.make_async_remote_copy(
                src_ref=packed_ref.at[there],
                dst_ref=got_ref.at[me],
                send_sem=send.at[k],
                recv_sem=recv.at[k],
                device_id={"obj": there},
                device_id_type=MESH,
            )
        )
    copies.append(pltpu.make_async_copy(packed_ref.at[me], got_ref.at[me], here.at[0]))
    copies.append(pltpu.make_async_copy(meta_ref.at[me], got_meta_ref.at[me], here.at[1]))
    for copy in copies:
        copy.start()
    for copy in copies:
        copy.wait()


def exchange(packed, meta):
    return pl.pallas_call(
        exchange_kernel,
        out_shape=(
            jax.ShapeDtypeStruct(packed.shape, F32),
            jax.ShapeDtypeStruct(meta.shape, jnp.int32),
        ),
        in_specs=[ANY, ANY],
        out_specs=(ANY, ANY),
        scratch_shapes=[pltpu.SemaphoreType.DMA((2,))] + [pltpu.SemaphoreType.DMA((OWNERS,))] * 4,
        compiler_params=pltpu.CompilerParams(collective_id=0, has_side_effects=True),
        name="exchange",
    )(packed, meta)


def update_kernel(meta_ref, amp_ref, object_ref, probe_ref, tables_ref, grad_ref, part_ref, strip, sem):
    slot = pl.program_id(0)
    group = lax.axis_index("pat")
    base = pl.multiple_of(jnp.minimum(group, 11) * STRIP, STRIP)

    @pl.when(slot == 0)
    def _():
        copies = []
        for block in range(BLOCKS):
            copies.append(
                pltpu.make_async_copy(
                    object_ref.at[:, pl.ds(base, SPAN), pl.ds(block * HALF, HALF)], strip.at[:, block], sem.at[block]
                )
            )
        for copy in copies:
            copy.start()
        grad_ref[...] = jnp.zeros_like(grad_ref)
        part_ref[...] = jnp.zeros_like(part_ref)
        for copy in copies:
            copy.wait()

    sender = slot // CAP
    place = 4 * (slot % CAP)

    @pl.when(meta_ref[sender, place, 0] > 0)
    def _():
        row = jnp.clip(meta_ref[sender, place + 1, 0] - base, 0, STRIP)
        col = meta_ref[sender, place + 2, 0]
        start = jnp.minimum(col // HALF, BLOCKS - 3)
        shift = col - start * HALF
        unshift = lax.rem(HALF - shift, HALF)
        lane = lax.broadcasted_iota(jnp.int32, (SIDE, HALF), 1)

        def window(part):
            turned = [
                pltpu.roll(strip[part, start + n, pl.ds(row, SIDE), :], unshift, axis=1) for n in range(3)
            ]
            inner = lane < HALF - shift
            return beside(jnp.where(inner, turned[0], turned[1]), jnp.where(inner, turned[1], turned[2]))

        probe_re = probe_ref[0]
        probe_im = probe_ref[1]
        window_re = window(0)
        window_im = window(1)
        exit_re = probe_re * window_re - probe_im * window_im
        exit_im = probe_re * window_im + probe_im * window_re

        def wanted_rows(parity):
            return by_parity(
                beside(
                    amp_ref[0, 0, 0, pl.ds(parity, HALF, stride=2), :],
                    amp_ref[0, 0, 1, pl.ds(parity, HALF, stride=2), :],
                )
            )

        res_re, res_im = residual_wave(
            exit_re, exit_im, wanted_rows, lambda i: (tables_ref[i, 0], tables_ref[i, 1])
        )
        part_ref[0] += window_re * res_re + window_im * res_im
        part_ref[1] += window_re * res_im - window_im * res_re

        def add(part, value):
            turn = lax.rem(shift, HALF)
            first = pltpu.roll(value[:, :HALF], turn, axis=1)
            second = pltpu.roll(value[:, HALF:], turn, axis=1)
            outer = lane >= shift
            grad_ref[part, start, pl.ds(row, SIDE), :] += jnp.where(outer, first, 0.0)
            grad_ref[part, start + 1, pl.ds(row, SIDE), :] += jnp.where(outer, second, first)
            grad_ref[part, start + 2, pl.ds(row, SIDE), :] += jnp.where(outer, 0.0, second)

        add(0, probe_re * res_re + probe_im * res_im)
        add(1, probe_re * res_im - probe_im * res_re)


def update(meta, amplitude, object_field, probe, tables):
    return pl.pallas_call(
        update_kernel,
        grid=(SLOTS,),
        out_shape=(
            jax.ShapeDtypeStruct((2, BLOCKS, SPAN, HALF), F32),
            jax.ShapeDtypeStruct((2, SIDE, SIDE), F32),
        ),
        in_specs=[
            SMEM,
            pl.BlockSpec((1, 1, 2, SIDE, HALF), lambda s: (s // CAP, s % CAP, 0, 0, 0)),
            ANY,
            pl.BlockSpec((2, SIDE, SIDE), lambda s: (0, 0, 0)),
            pl.BlockSpec(tables.shape, lambda s: (0, 0, 0, 0)),
        ],
        out_specs=(
            pl.BlockSpec((2, BLOCKS, SPAN, HALF), lambda s: (0, 0, 0, 0)),
            pl.BlockSpec((2, SIDE, SIDE), lambda s: (0, 0, 0)),
        ),
        scratch_shapes=[pltpu.VMEM((2, BLOCKS, SPAN, HALF), F32), pltpu.SemaphoreType.DMA((BLOCKS,))],
        compiler_params=pltpu.CompilerParams(
            vmem_limit_bytes=48 * 2**20, dimension_semantics=("arbitrary",)
        ),
        name="update",
    )(meta, amplitude, object_field, probe, tables)


def combine_kernel(
    grad_ref, part_ref, out_ref, probe_ref,
    own, rise, got_x, got_y, near, quarter, sixteenth,
    load, send_x, recv_x, send_y, recv_y,
    send_a, recv_a, send_b, recv_b, send_c, recv_c, send_d, recv_d, send_e, recv_e,
):
    me = lax.axis_index("obj")
    group = lax.axis_index("pat")
    x = lax.rem(group, NX)
    y = group // NX
    last = y == NY - 1

    def obj_peer(k):
        return {"obj": lax.rem(me + k, OWNERS)}

    def x_peer(k):
        return {"pat": y * NX + lax.rem(x + k, NX)}

    def y_peer(k):
        return {"pat": lax.rem(y + k, NY) * NX + x}

    peers = [obj_peer(k) for k in range(1, OWNERS)]
    peers += [x_peer(k) for k in range(1, NX)] + [y_peer(k) for k in range(1, NY)]
    barrier = pltpu.get_barrier_semaphore()
    for peer in peers:
        pl.semaphore_signal(barrier, inc=1, device_id=peer, device_id_type=MESH)

    def block(number):
        return pl.ds(pl.multiple_of(number * STRIP, STRIP), STRIP)

    def lanes(c):
        return pl.ds(c * CHUNK, CHUNK)

    own_block = jnp.where(last, x + 1, 0)
    load_own = pltpu.make_async_copy(grad_ref.at[:, :, block(own_block), :], own, load.at[0])
    load_rise = pltpu.make_async_copy(grad_ref.at[:, :, block(4), :], rise, load.at[1])
    load_own.start()
    load_rise.start()
    pl.semaphore_wait(barrier, len(peers))

    def remote(src, dst, send, recv, peer):
        return pltpu.make_async_remote_copy(
            src_ref=src, dst_ref=dst, send_sem=send, recv_sem=recv, device_id=peer, device_id_type=MESH
        )

    def eighth(number):
        return pl.ds(pl.multiple_of(number * 64, 64), 64)

    stage_a = []
    for k in range(1, OWNERS):
        there = lax.rem(me + k, OWNERS)
        stage_a.append(
            remote(part_ref.at[eighth(there)], near.at[k], send_a.at[k], recv_a.at[k], obj_peer(k))
        )
    for copy in stage_a:
        copy.start()

    stage_x = {}
    for c in range(CHUNKS):
        for k in range(1, NX):
            there = lax.rem(x + k, NX)
            number = jnp.where(last, there + 1, k)
            stage_x[c, k] = remote(
                grad_ref.at[:, lanes(c), block(number), :],
                got_x.at[k - 1, :, lanes(c)],
                send_x.at[k - 1, c],
                recv_x.at[k - 1, c],
                x_peer(k),
            )
            stage_x[c, k].start()

    for copy in stage_a:
        copy.wait()
    total = part_ref[eighth(me), :]
    for k in range(1, OWNERS):
        total = total + near[k]
    near[0] = total

    def sixteen(number):
        return pl.ds(pl.multiple_of(number * 16, 16), 16)

    stage_b = []
    for k in range(1, NX):
        there = lax.rem(x + k, NX)
        stage_b.append(
            remote(near.at[0, sixteen(there), :], quarter.at[k], send_b.at[k], recv_b.at[k], x_peer(k))
        )
    for copy in stage_b:
        copy.start()
    for copy in stage_b:
        copy.wait()
    total = near[0, sixteen(x), :]
    for k in range(1, NX):
        total = total + quarter[k]
    sixteenth[y] = total
    stage_c = []
    for k in range(1, NY):
        stage_c.append(
            remote(sixteenth.at[y], sixteenth.at[y], send_c.at[k], recv_c.at[k], y_peer(k))
        )
    for copy in stage_c:
        copy.start()
    for copy in stage_c:
        copy.wait()
    total = (sixteenth[0] + sixteenth[1]) + (sixteenth[2] + sixteenth[3])
    mine = pl.ds(pl.multiple_of(me * 64 + x * 16, 16), 16)
    probe_ref[mine, :] = total * (1.0 / math.sqrt(1024.0))
    stage_d = []
    for k in range(1, NX):
        stage_d.append(
            remote(probe_ref.at[mine], probe_ref.at[mine], send_d.at[k], recv_d.at[k], x_peer(k))
        )
    for copy in stage_d:
        copy.start()
    for copy in stage_d:
        copy.wait()
    stage_e = []
    for k in range(1, OWNERS):
        stage_e.append(
            remote(
                probe_ref.at[eighth(me)], probe_ref.at[eighth(me)], send_e.at[k], recv_e.at[k], obj_peer(k)
            )
        )
    for copy in stage_e:
        copy.start()

    load_own.wait()
    load_rise.wait()
    stage_y = []
    for c in range(CHUNKS):
        for k in range(1, NX):
            stage_x[c, k].wait()
        mine_too = own[:, lanes(c)]
        above_too = rise[:, lanes(c)]
        for k in range(1, NX):
            arrived = got_x[k - 1, :, lanes(c)]
            here = (k <= x) | last
            mine_too = mine_too + jnp.where(here, arrived, 0.0)
            above_too = above_too + jnp.where(here, 0.0, arrived)
        own[:, lanes(c)] = mine_too
        rise[:, lanes(c)] = above_too
        copy = remote(
            rise.at[:, lanes(c)], got_y.at[:, lanes(c)], send_y.at[c], recv_y.at[c], y_peer(1)
        )
        stage_y.append(copy)

        @pl.when(y < NY - 1)
        def _():
            copy.start()

    for c in range(CHUNKS):

        @pl.when(y > 0)
        def _():
            stage_y[c].wait_recv()
            for n in range(c * CHUNK, (c + 1) * CHUNK):
                out_ref[:, :, pl.ds(n * HALF, HALF)] = own[:, n] + got_y[:, n]

        @pl.when(y == 0)
        def _():
            for n in range(c * CHUNK, (c + 1) * CHUNK):
                out_ref[:, :, pl.ds(n * HALF, HALF)] = own[:, n]

    @pl.when(y < NY - 1)
    def _():
        for copy in stage_y:
            copy.wait_send()

    for copy in stage_e:
        copy.wait()


def combine(gradient, probe_part):
    dma = pltpu.SemaphoreType.DMA
    return pl.pallas_call(
        combine_kernel,
        out_shape=(
            jax.ShapeDtypeStruct((2, STRIP, TILE), F32),
            jax.ShapeDtypeStruct((2 * SIDE, SIDE), F32),
        ),
        in_specs=[ANY, VMEM],
        out_specs=(VMEM, VMEM),
        scratch_shapes=[
            pltpu.VMEM((2, BLOCKS, STRIP, HALF), F32),
            pltpu.VMEM((2, BLOCKS, STRIP, HALF), F32),
            pltpu.VMEM((NX - 1, 2, BLOCKS, STRIP, HALF), F32),
            pltpu.VMEM((2, BLOCKS, STRIP, HALF), F32),
            pltpu.VMEM((OWNERS, 64, SIDE), F32),
            pltpu.VMEM((NX, 16, SIDE), F32),
            pltpu.VMEM((NY, 16, SIDE), F32),
            dma((2,)),
            dma((NX - 1, CHUNKS)),
            dma((NX - 1, CHUNKS)),
            dma((CHUNKS,)),
            dma((CHUNKS,)),
            dma((OWNERS,)),
            dma((OWNERS,)),
            dma((NX,)),
            dma((NX,)),
            dma((NY,)),
            dma((NY,)),
            dma((NX,)),
            dma((NX,)),
            dma((OWNERS,)),
            dma((OWNERS,)),
        ],
        compiler_params=pltpu.CompilerParams(
            collective_id=1, has_side_effects=True, vmem_limit_bytes=32 * 2**20
        ),
        name="combine",
    )(gradient, probe_part.reshape(2 * SIDE, SIDE))


def on_device(object_field, probe, amplitude, tile_owner, row_start, col_start):
    tables = jnp.asarray(dft_tables())
    packed, meta = pack(tile_owner, row_start, col_start, amplitude)
    got, got_meta = exchange(packed, meta)
    gradient, probe_part = update(got_meta, got, object_field, probe, tables)
    object_grad, probe_grad = combine(gradient, probe_part)
    return object_grad, probe_grad.reshape(2, SIDE, SIDE)


def solution(mesh):
    return jax.shard_map(
        on_device,
        mesh=mesh,
        in_specs=(
            P(None, None, "obj"),
            P(),
            P(("pat", "obj"), None, None),
            P(("pat", "obj"), None),
            P(("pat", "obj")),
            P(("pat", "obj")),
        ),
        out_specs=(P(None, "pat", "obj"), P()),
        check_vma=False,
    )
```

time: 842 us -> 244 us (0.29)
  waiting for transfers between devices: 302 us -> 0 us
  Pallas kernels: 0 us -> 234 us
  local copies, waits for them, and re-layouts: 212 us -> 6.48 us
  matrix products: 167 us -> 0 us
  loops' own time: 60.7 us -> 0 us
  other arithmetic: 52.1 us -> 0 us
  starting transfers between devices: 22.2 us -> 0 us
  between operations: 16.2 us -> 0.71 us
    pallas_call x0 -> x4, Pallas kernels: none -> 234 us  [the longest x1 87.6 us: combine(): pl.pallas_call(combine_kernel, out_shape=(jax.ShapeDtypeStruct((2, STRIP,...]
    all_to_all x4 -> x0, waiting for transfers between devices: 190 us -> none  [the longest x1 91.9 us: on_device(): lax.all_to_all(by_owner(local_res), 'obj', split_axis=0, concat_axis=0, t...]
    dot_general x18 -> x0, matrix products: 167 us -> none  [the longest x2 21.8 us: both_sides(): jnp.einsum('sjk,kl->sjl', left_re, table_im, precision=high)]
    reduce_scatter x1 -> x0, waiting for transfers between devices: 113 us -> none  [on_device(): lax.psum_scatter(gradient, 'pat', scatter_dimension=1, tiled=True)]
    dynamic_update_slice x16 -> x0, local copies, waits for them, and re-layouts: 101 us -> none  [add_window(): return lax.dynamic_update_slice(gradient, before + update[number], corner)]
    gather x48 -> x0, local copies, waits for them, and re-layouts: 64.9 us -> none
    another operation x2 -> x0, loops' own time: 60.7 us -> none  [the longest x1 60.6 us: on_device(): lax.fori_loop(0, slots, add_window, jnp.zeros(object_field.shape, jnp.flo...]
    add x16 -> x0, other arithmetic: 24.5 us -> none  [add_window(): return lax.dynamic_update_slice(gradient, before + update[number], corner)]
  transfers between devices with their start and end apart: 6 -> 0, of which waited for: 5 -> 0; matrix products, arithmetic and copies ran while one was open for 20% -> 0% of each run, Pallas kernels for 0% -> 0%
where the time goes in v1:
time: 244 us; the launch traced here: 241 us
  Pallas kernels  234 us (96%)
  local copies, waits for them, and re-layouts  6.48 us (3%)
    pallas_call x1, Pallas kernels, combine(): pl.pallas_call(combine_kernel, out_shape=(jax.ShapeDtypeStruct((2, STRIP,...  87.6 us
    pallas_call x1, Pallas kernels, pack(): pl.pallas_call(pack_kernel, out_shape=(jax.ShapeDtypeStruct((OWNERS, CAP,...  66.1 us
    pallas_call x1, Pallas kernels, exchange(): pl.pallas_call(exchange_kernel, out_shape=(jax.ShapeDtypeStruct(packed.sh...  53.4 us
    pallas_call x1, Pallas kernels, update(): pl.pallas_call(update_kernel, grid=(SLOTS,), out_shape=(jax.ShapeDtypeStr...  26.7 us
    unnamed x11, local copies, waits for them, and re-layouts  6.48 us

profile of v1, /device:TPU:1, one launch (start us, length us, event | category | flops | bytes accessed | tf_op | source)
XLA Modules:
  0.0 241.0 jit_solution(7738834327612969671)
XLA Ops:
  0.6 0.0 copy-start.1
  0.6 0.0 copy-start.2
  0.7 1.5 copy.9.owner_ref
  2.1 66.1 %pack.1 = (f32[8,2,2,256,128]{4,3,2,1,0:T(8,128)}, s32[8,8,128]{2,1,0:T(8,128)}) custom-call(s32[8,1]{1,0:T(8,128)} %copy.9.owner_ref, s32[8]{0:T(128)} %row_ref.1, s32[8]{0:T(128)} %col_ref.1, f32[8,256,256]{2,1,0:T(8,128)} %amp_ref.1), custom_call_target="tpu_custom_call" | custom-call | tf_op jit(solution)/shard_map/pack/pallas_call | solution.py:160
  68.3 53.4 %exchange.1 = (f32[8,2,2,256,128]{4,3,2,1,0:T(8,128)}, s32[8,8,128]{2,1,0:T(8,128)}) custom-call(f32[8,2,2,256,128]{4,3,2,1,0:T(8,128)} %get-tuple-element.10.packed_ref, s32[8,8,128]{2,1,0:T(8,128)} %get-tuple-element.11.meta_ref), custom_call_target="tpu_custom_call" | custom-call | tf_op jit(solution)/shard_map/exchange/pallas_call | solution.py:213
  121.6 0.0 copy-done.1
  121.7 0.0 copy-done.2
  121.7 0.0 copy-start.3
  121.7 0.7 copy-done.3
  122.4 26.7 %update.1 = (f32[2,16,320,128]{3,2,1,0:T(8,128)}, f32[2,256,256]{2,1,0:T(8,128)S(1)}) custom-call(s32[8,8,128]{2,1,0:T(8,128)S(1)} %copy-done.3, f32[8,2,2,256,128]{4,3,2,1,0:T(8,128)} %get-tuple-element.13.amp_ref, f32[2,1024,2048]{2,1,0:T(8,128)} %object_ref.1, f32[2,256,256]{2,1,0:T(8,128)S(1)} %copy-done.2, bf16[8,2,256,256]{3,2,1,0:T(8,128)(2,1)S(1)} %copy-done.1), custom_call_target="tpu_custom_call" | custom-call | tf_op jit(solution)/shard_map/update/pallas_call | solution.py:302
  149.1 0.0 copy-start
  149.1 2.5 %copy-done = f32[2,16,320,128]{3,2,1,0:T(8,128)S(1)} copy-done((f32[2,16,320,128]{3,2,1,0:T(8,128)S(1)}, f32[2,16,320,128]{3,2,1,0:T(8,128)}, u32[]{:S(2)}) %copy-start) | copy-done | bytes 5242904
  151.6 87.6 %combine.1 = (f32[2,64,2048]{2,1,0:T(8,128)S(1)}, f32[512,256]{1,0:T(8,128)S(1)}) custom-call(f32[2,16,320,128]{3,2,1,0:T(8,128)S(1)} %copy-done, f32[512,256]{1,0:T(8,128)S(1)} %bitcast.3), custom_call_target="tpu_custom_call" | custom-call | tf_op jit(solution)/shard_map/combine/pallas_call | solution.py:502
  239.3 1.0 copy.12
  240.2 0.8 copy.13
Async XLA Ops:
  0.6 121.0 %copy-start.1 = (bf16[8,2,256,256]{3,2,1,0:T(8,128)(2,1)S(1)}, bf16[8,2,256,256]{3,2,1,0:T(8,128)(2,1)}, u32[]{:S(2)}) copy-start(bf16[8,2,256,256]{3,2,1,0:T(8,128)(2,1)} %constant.2.clone.tables_ref) | copy-start | bytes 6291460
  0.6 121.0 %copy-start.2 = (f32[2,256,256]{2,1,0:T(8,128)S(1)}, f32[2,256,256]{2,1,0:T(8,128)}, u32[]{:S(2)}) copy-start(f32[2,256,256]{2,1,0:T(8,128)} %probe_ref.1) | copy-start | bytes 1572868
  121.7 0.8 copy-start.3
  149.1 2.5 %copy-start = (f32[2,16,320,128]{3,2,1,0:T(8,128)S(1)}, f32[2,16,320,128]{3,2,1,0:T(8,128)}, u32[]{:S(2)}) copy-start(f32[2,16,320,128]{3,2,1,0:T(8,128)} %get-tuple-element.14.grad_ref) | copy-start | bytes 15728644

commit v2 on v0

v2 whole, which is shorter than its diff:
```python
import math

import jax
import jax.numpy as jnp
import numpy as np
from jax import lax
from jax.experimental import pallas as pl
from jax.experimental.pallas import tpu as pltpu
from jax.sharding import PartitionSpec as P

MESH = pl.DeviceIdType.MESH
CAP = 2
SIDE = 256
HALF = 128
STRIP = 64
SPAN = 320
TILE = 2048
BLOCKS = TILE // HALF
SOFTEN = 0.25
OWNERS = 8
COUNT = 8
SLOTS = OWNERS * CAP
NX = 4
NY = 4
CHUNKS = 8
CHUNK = BLOCKS // CHUNKS
F32 = jnp.float32
BF16 = jnp.bfloat16
ANY = pl.BlockSpec(memory_space=pl.ANY)
VMEM = pl.BlockSpec(memory_space=pltpu.VMEM)
SMEM = pl.BlockSpec(memory_space=pltpu.SMEM)


def dft_tables():
    index = np.arange(SIDE)
    full = np.exp(-2j * np.pi * (np.outer(index, index) % SIDE) / SIDE) / math.sqrt(SIDE)

    def right(table):
        return np.block([[table.real, table.imag], [-table.imag, table.real]])

    swap = np.roll(np.arange(HALF), -HALF // 2)
    half = [full[:HALF, 0::2], full[:HALF, 1::2]]
    lane = [half[0], half[1][:, swap]]
    tables = [
        right(lane[0]),
        right(lane[1]),
        right(half[0]).T,
        right(half[1]).T,
        right(half[0].conj().T).T,
        right(half[1].conj().T).T,
        right(lane[0].conj().T),
        right(lane[1].conj().T),
    ]
    exact = np.stack(tables).astype(np.float32)
    high = exact.astype(BF16)
    low = (exact - high.astype(np.float32)).astype(BF16)
    return np.stack([high, low], axis=1)


def split(value):
    high = value.astype(BF16)
    return high, (value - high.astype(F32)).astype(BF16)


def times_table(data, table):
    high, low = split(data)
    left = jnp.concatenate([high, low, high], axis=1)
    right = jnp.concatenate([table[0], table[0], table[1]], axis=0)
    return jnp.dot(left, right, preferred_element_type=F32)


def table_times(table, data):
    high, low = split(data)
    left = jnp.concatenate([table[0], table[0], table[1]], axis=1)
    right = jnp.concatenate([high, low, high], axis=0)
    return jnp.dot(left, right, preferred_element_type=F32)


def beside(*parts):
    return jnp.concatenate(parts, axis=1)


def above(*parts):
    return jnp.concatenate(parts, axis=0)


def by_parity(rows):
    lane = lax.broadcasted_iota(jnp.int32, (HALF, HALF), 1)
    front = lane < HALF // 2
    first = jnp.take_along_axis(
        rows[:, :HALF], jnp.where(front, 2 * lane, 2 * lane - HALF + 1), axis=1, mode="promise_in_bounds"
    )
    second = jnp.take_along_axis(
        rows[:, HALF:], jnp.where(front, 2 * lane + 1, 2 * lane - HALF), axis=1, mode="promise_in_bounds"
    )
    return beside(jnp.where(front, first, second), jnp.where(front, second, first))


FRONT = slice(0, HALF)
BACK = slice(HALF, SIDE)


def residual_waves(exits, wanted_rows, tables):
    count = len(exits)

    def from_right(waves, number):
        out = times_table(above(*waves), tables(number))
        return [out[SIDE * j : SIDE * (j + 1)] for j in range(count)]

    def from_left(number, waves):
        out = table_times(tables(number), beside(*waves))
        return [out[:, SIDE * j : SIDE * (j + 1)] for j in range(count)]

    even = from_right(
        [beside(re[:, FRONT] + re[:, BACK], im[:, FRONT] + im[:, BACK]) for re, im in exits], 0
    )
    odd = from_right(
        [beside(re[:, FRONT] - re[:, BACK], im[:, FRONT] - im[:, BACK]) for re, im in exits], 1
    )
    half_re = [beside(e[:, FRONT], o[:, FRONT]) for e, o in zip(even, odd)]
    half_im = [beside(e[:, BACK], o[:, BACK]) for e, o in zip(even, odd)]
    pairs = list(zip(half_re, half_im))
    spectrum = [
        from_left(2, [above(re[FRONT] + re[BACK], im[FRONT] + im[BACK]) for re, im in pairs]),
        from_left(3, [above(re[FRONT] - re[BACK], im[FRONT] - im[BACK]) for re, im in pairs]),
    ]
    returned = []
    for parity in range(2):
        scaled = []
        for j in range(count):
            re, im = spectrum[parity][j][FRONT], spectrum[parity][j][BACK]
            ratio = wanted_rows(j, parity) * lax.rsqrt(re * re + im * im + SOFTEN)
            scaled.append(above(re * ratio, im * ratio))
        returned.append(from_left(4 + parity, scaled))
    pairs = []
    for e, o in zip(*returned):
        re = above(e[FRONT] + o[FRONT], e[FRONT] - o[FRONT])
        im = above(e[BACK] + o[BACK], e[BACK] - o[BACK])
        pairs.append((re, im))
    even = from_right([beside(re[:, FRONT], im[:, FRONT]) for re, im in pairs], 6)
    odd = from_right([beside(re[:, BACK], im[:, BACK]) for re, im in pairs], 7)
    residuals = []
    for (re, im), e, o in zip(exits, even, odd):
        back_re = beside(e[:, FRONT] + o[:, FRONT], e[:, FRONT] - o[:, FRONT])
        back_im = beside(e[:, BACK] + o[:, BACK], e[:, BACK] - o[:, BACK])
        residuals.append((back_re - re, back_im - im))
    return residuals


def pack_kernel(owner_ref, row_ref, col_ref, amp_ref, packed_ref, meta_ref, held, come, leave):
    def arriving(j, side):
        return pltpu.make_async_copy(
            amp_ref.at[j, :, pl.ds(side * HALF, HALF)], held.at[j, side], come.at[j, side]
        )

    for j in range(COUNT):
        for side in range(2):
            arriving(j, side).start()
    ranks = []
    for j in range(COUNT):
        rank = jnp.int32(0)
        for i in range(j):
            rank = rank + (owner_ref[i, 0] == owner_ref[j, 0]).astype(jnp.int32)
        ranks.append(rank)
    leaving = []
    for j in range(COUNT):
        for side in range(2):
            arriving(j, side).wait()
        copy = pltpu.make_async_copy(held.at[j], packed_ref.at[owner_ref[j, 0], ranks[j]], leave.at[j])
        copy.start()
        leaving.append(copy)
    meta_ref[...] = jnp.zeros_like(meta_ref)
    sub = lax.broadcasted_iota(jnp.int32, (8, 128), 0)
    for j in range(COUNT):
        mine = (sub // 4 == ranks[j]) & (sub % 4 < 3)
        value = jnp.where(sub % 4 == 0, 1, jnp.where(sub % 4 == 1, row_ref[j], col_ref[j]))
        meta_ref[owner_ref[j, 0]] = jnp.where(mine, value, meta_ref[owner_ref[j, 0]])
    for copy in leaving:
        copy.wait()


def pack(tile_owner, row_start, col_start, amplitude):
    return pl.pallas_call(
        pack_kernel,
        out_shape=(
            jax.ShapeDtypeStruct((OWNERS, CAP, 2, SIDE, HALF), F32),
            jax.ShapeDtypeStruct((OWNERS, 8, 128), jnp.int32),
        ),
        in_specs=[SMEM, SMEM, SMEM, ANY],
        out_specs=(ANY, VMEM),
        scratch_shapes=[
            pltpu.VMEM((COUNT, 2, SIDE, HALF), F32),
            pltpu.SemaphoreType.DMA((COUNT, 2)),
            pltpu.SemaphoreType.DMA((COUNT,)),
        ],
        name="pack",
    )(tile_owner, row_start, col_start, amplitude)


def step_kernel(
    packed_ref, meta_ref, object_ref, probe_ref, tables_ref, out_ref, total_ref,
    got, got_meta, corners, strip, tables, pads, part, grad, got_x, got_y, own, rise, near, quarter, sixteenth,
    load, send, recv, send_meta, recv_meta, send_x, recv_x, send_y, recv_y,
    send_a, recv_a, send_b, recv_b, send_c, recv_c, send_d, recv_d, send_e, recv_e,
):
    me = lax.axis_index("obj")
    z = me // 2
    core = lax.rem(me, 2)
    group = lax.axis_index("pat")
    x = lax.rem(group, NX)
    y = group // NX
    last = y == NY - 1
    base = pl.multiple_of(jnp.minimum(group, 11) * STRIP, STRIP)

    def obj_at(r):
        return lax.rem(z + r // 2, OWNERS // 2) * 2 + lax.rem(core + lax.rem(r, 2), 2)

    def obj_peer(r):
        return {"obj": obj_at(r)}

    def x_peer(k):
        return {"pat": y * NX + lax.rem(x + k, NX)}

    def y_peer(k):
        return {"pat": lax.rem(y + k, NY) * NX + x}

    def remote(src, dst, send, recv, peer):
        return pltpu.make_async_remote_copy(
            src_ref=src, dst_ref=dst, send_sem=send, recv_sem=recv, device_id=peer, device_id_type=MESH
        )

    peers = [obj_peer(r) for r in range(1, OWNERS)]
    peers += [x_peer(k) for k in range(1, NX)] + [y_peer(k) for k in range(1, NY)]
    barrier = pltpu.get_barrier_semaphore()
    for peer in peers:
        pl.semaphore_signal(barrier, inc=1, device_id=peer, device_id_type=MESH)

    loads = [
        pltpu.make_async_copy(
            object_ref.at[:, pl.ds(base, SPAN), pl.ds(n * HALF, HALF)], strip.at[:, n], load.at[n]
        )
        for n in range(BLOCKS)
    ]
    loads.append(pltpu.make_async_copy(tables_ref, tables, load.at[BLOCKS]))
    load_meta = pltpu.make_async_copy(meta_ref.at[me], got_meta.at[0], load.at[BLOCKS + 1])
    load_own = pltpu.make_async_copy(packed_ref.at[me], got.at[0], load.at[BLOCKS + 2])

    def metas(r):
        return remote(meta_ref.at[obj_at(r)], got_meta.at[r], send_meta.at[r], recv_meta.at[r], obj_peer(r))

    def amplitudes(r):
        return remote(packed_ref.at[obj_at(r)], got.at[r], send.at[r], recv.at[r], obj_peer(r))

    load_meta.start()
    pl.semaphore_wait(barrier, len(peers))
    for r in range(1, OWNERS):
        metas(r).start()
    amplitudes(1).start()
    for dz in (1, 3, 2):
        amplitudes(2 * dz + core).start()
    load_own.start()
    for copy in loads:
        copy.start()
    edge = jnp.zeros((2, STRIP, HALF), F32)
    for n in range(3 * SLOTS):
        pads[n, :, pl.ds(0, STRIP), :] = edge
        pads[n, :, pl.ds(STRIP + SIDE, STRIP), :] = edge
    pads[3 * SLOTS] = jnp.zeros((2, SPAN + STRIP, HALF), F32)
    part[...] = jnp.zeros_like(part)
    load_meta.wait()
    for r in range(1, OWNERS):
        metas(r).wait_recv()
    load_corners = pltpu.make_async_copy(got_meta, corners, load.at[BLOCKS + 3])
    load_corners.start()
    load_corners.wait()
    for copy in loads:
        copy.wait()
    load_own.wait()

    lane = lax.broadcasted_iota(jnp.int32, (SIDE, HALF), 1)

    def corner(slot):
        r = slot // CAP
        at = 4 * lax.rem(slot, CAP)
        row = jnp.clip(corners[r, at + 1, 0] - base, 0, STRIP)
        col = jnp.clip(corners[r, at + 2, 0], 0, TILE - SIDE)
        start = jnp.minimum(col // HALF, BLOCKS - 3)
        return row, start, col - start * HALF

    def window(slot, part):
        row, start, shift = corner(slot)
        unshift = lax.rem(HALF - shift, HALF)
        turned = [
            pltpu.roll(strip[part, start + n, pl.ds(row, SIDE), :], unshift, axis=1) for n in range(3)
        ]
        inner = lane < HALF - shift
        return beside(jnp.where(inner, turned[0], turned[1]), jnp.where(inner, turned[1], turned[2]))

    def from_source(k, carry):
        r = jnp.where(k < 4, k, jnp.where(k < 6, k + 2, k - 2))

        @pl.when(k == jnp.where(core == 0, 6, 2))
        def _():
            for dz in (1, 3, 2):
                amplitudes(2 * dz + core).wait_send()
            for dz in (1, 3, 2):
                amplitudes(2 * dz + 1 - core).start()

        @pl.when(k > 0)
        def _():
            amplitudes(r).wait_recv()

        slots = [CAP * r + n for n in range(CAP)]
        probe_re = probe_ref[0]
        probe_im = probe_ref[1]
        windows = [(window(slot, 0), window(slot, 1)) for slot in slots]
        exits = [
            (probe_re * re - probe_im * im, probe_re * im + probe_im * re) for re, im in windows
        ]

        def wanted_rows(j, parity):
            return by_parity(
                beside(
                    got[r, j, 0, pl.ds(parity, HALF, stride=2), :],
                    got[r, j, 1, pl.ds(parity, HALF, stride=2), :],
                )
            )

        residuals = residual_waves(exits, wanted_rows, lambda i: (tables[i, 0], tables[i, 1]))
        part_re = part[pl.ds(0, SIDE), :]
        part_im = part[pl.ds(SIDE, SIDE), :]
        for j, slot in enumerate(slots):
            keep = corners[r, 4 * j, 0] > 0
            res_re = jnp.where(keep, residuals[j][0], 0.0)
            res_im = jnp.where(keep, residuals[j][1], 0.0)
            window_re, window_im = windows[j]
            part_re = part_re + (window_re * res_re + window_im * res_im)
            part_im = part_im + (window_re * res_im - window_im * res_re)
            shift = corner(slot)[2]
            turn = lax.rem(shift, HALF)
            outer = lane >= shift
            rows = pl.ds(STRIP, SIDE)
            for c, value in (
                (0, probe_re * res_re + probe_im * res_im),
                (1, probe_re * res_im - probe_im * res_re),
            ):
                first = pltpu.roll(value[:, FRONT], turn, axis=1)
                second = pltpu.roll(value[:, BACK], turn, axis=1)
                pads[3 * slot, c, rows, :] = jnp.where(outer, first, 0.0)
                pads[3 * slot + 1, c, rows, :] = jnp.where(outer, second, first)
                pads[3 * slot + 2, c, rows, :] = jnp.where(outer, 0.0, second)
        part[pl.ds(0, SIDE), :] = part_re
        part[pl.ds(SIDE, SIDE), :] = part_im
        return carry

    lax.fori_loop(0, OWNERS, from_source, 0)

    def eighth(number):
        return pl.ds(pl.multiple_of(number * 64, 64), 64)

    def sixteen(number):
        return pl.ds(pl.multiple_of(number * 16, 16), 16)

    mine = pl.ds(pl.multiple_of(me * 64 + y * 16, 16), 16)

    def stage_a(r):
        return remote(part.at[eighth(obj_at(r))], near.at[r], send_a.at[r], recv_a.at[r], obj_peer(r))

    def stage_b(k):
        there = lax.rem(y + k, NY)
        return remote(near.at[0, sixteen(there)], quarter.at[k], send_b.at[k], recv_b.at[k], y_peer(k))

    def stage_c(k):
        return remote(sixteenth.at[x], sixteenth.at[x], send_c.at[k], recv_c.at[k], x_peer(k))

    def stage_d(k):
        return remote(total_ref.at[mine], total_ref.at[mine], send_d.at[k], recv_d.at[k], y_peer(k))

    def stage_e(r):
        return remote(
            total_ref.at[eighth(me)], total_ref.at[eighth(me)], send_e.at[r], recv_e.at[r], obj_peer(r)
        )

    def probe_step(number):
        if number == 0:
            for r in range(1, OWNERS):
                stage_a(r).wait()
            value = part[eighth(me), :]
            for r in range(1, OWNERS):
                value = value + near[r]
            near[0] = value
            for k in range(1, NY):
                stage_b(k).start()
        elif number == 1:
            for k in range(1, NY):
                stage_b(k).wait()
            value = near[0, sixteen(y), :]
            for k in range(1, NY):
                value = value + quarter[k]
            sixteenth[x] = value
            for k in range(1, NX):
                stage_c(k).start()
        elif number == 2:
            for k in range(1, NX):
                stage_c(k).wait()
            value = (sixteenth[0] + sixteenth[1]) + (sixteenth[2] + sixteenth[3])
            total_ref[mine, :] = value * (1.0 / math.sqrt(1024.0))
            for k in range(1, NY):
                stage_d(k).start()
        elif number == 3:
            for k in range(1, NY):
                stage_d(k).wait()
            for r in range(1, OWNERS):
                stage_e(r).start()
        else:
            for r in range(1, OWNERS):
                stage_e(r).wait()

    for r in range(1, OWNERS):
        stage_a(r).start()

    def block(number):
        return pl.ds(pl.multiple_of(number * STRIP, STRIP), STRIP)

    def along_x(c, k):
        number = jnp.where(last, lax.rem(x + k, NX) + 1, k)
        columns = pl.ds(c * CHUNK, CHUNK)
        return remote(
            grad.at[:, columns, block(number)],
            got_x.at[k - 1, :, columns],
            send_x.at[k - 1, c],
            recv_x.at[k - 1, c],
            x_peer(k),
        )

    def along_y(c):
        columns = pl.ds(c * CHUNK, CHUNK)
        return remote(rise.at[:, columns], got_y.at[:, columns], send_y.at[c], recv_y.at[c], y_peer(1))

    def gather_chunk(c, carry):
        def gather_block(b, carry):
            for part in range(2):
                value = None
                for slot in range(SLOTS):
                    row, start, _ = corner(slot)
                    n = b - start
                    at = jnp.where((n >= 0) & (n < 3), 3 * slot + n, 3 * SLOTS)
                    term = pads[at, part, pl.ds(STRIP - row, SPAN), :]
                    value = term if value is None else value + term
                grad[part, b] = value
            return carry

        lax.fori_loop(c * CHUNK, (c + 1) * CHUNK, gather_block, 0)
        for k in range(1, NX):
            along_x(c, k).start()
        return carry

    lax.fori_loop(0, CHUNKS, gather_chunk, 0)

    own_block = block(jnp.where(last, x + 1, 0))
    for c in range(CHUNKS):
        columns = pl.ds(c * CHUNK, CHUNK)
        for k in range(1, NX):
            along_x(c, k).wait_recv()
        here_too = grad[:, columns, own_block, :]
        above_too = grad[:, columns, block(4), :]
        for k in range(1, NX):
            arrived = got_x[k - 1, :, columns]
            here = (k <= x) | last
            here_too = here_too + jnp.where(here, arrived, 0.0)
            above_too = above_too + jnp.where(here, 0.0, arrived)
        own[:, columns] = here_too
        rise[:, columns] = above_too

        @pl.when(y < NY - 1)
        def _():
            along_y(c).start()

        if c in (1, 3, 5, 6):

            @pl.when(core == 1)
            def _():
                probe_step((1, 3, 5, 6).index(c))

    for c in range(CHUNKS):

        @pl.when(y > 0)
        def _():
            along_y(c).wait_recv()
            for n in range(c * CHUNK, (c + 1) * CHUNK):
                out_ref[:, :, pl.ds(n * HALF, HALF)] = own[:, n] + got_y[:, n]

        @pl.when(y == 0)
        def _():
            for n in range(c * CHUNK, (c + 1) * CHUNK):
                out_ref[:, :, pl.ds(n * HALF, HALF)] = own[:, n]

        @pl.when(y < NY - 1)
        def _():
            along_y(c).wait_send()

    @pl.when(core == 0)
    def _():
        for number in range(4):
            probe_step(number)

    for r in range(1, OWNERS):
        metas(r).wait_send()
    amplitudes(1).wait_send()
    for dz in (1, 3, 2):
        amplitudes(2 * dz + 1 - core).wait_send()
    for c in range(CHUNKS):
        for k in range(1, NX):
            along_x(c, k).wait_send()
    probe_step(4)


def step(packed, meta, object_field, probe, tables):
    dma = pltpu.SemaphoreType.DMA
    return pl.pallas_call(
        step_kernel,
        out_shape=(
            jax.ShapeDtypeStruct((2, STRIP, TILE), F32),
            jax.ShapeDtypeStruct((2 * SIDE, SIDE), F32),
        ),
        in_specs=[ANY, VMEM, ANY, VMEM, ANY],
        out_specs=(VMEM, VMEM),
        scratch_shapes=[
            pltpu.VMEM((OWNERS, CAP, 2, SIDE, HALF), F32),
            pltpu.VMEM((OWNERS, 8, 128), jnp.int32),
            pltpu.SMEM((OWNERS, 8, 128), jnp.int32),
            pltpu.VMEM((2, BLOCKS, SPAN, HALF), F32),
            pltpu.VMEM(tables.shape, BF16),
            pltpu.VMEM((3 * SLOTS + 1, 2, SPAN + STRIP, HALF), F32),
            pltpu.VMEM((2 * SIDE, SIDE), F32),
            pltpu.VMEM((2, BLOCKS, SPAN, HALF), F32),
            pltpu.VMEM((NX - 1, 2, BLOCKS, STRIP, HALF), F32),
            pltpu.VMEM((2, BLOCKS, STRIP, HALF), F32),
            pltpu.VMEM((2, BLOCKS, STRIP, HALF), F32),
            pltpu.VMEM((2, BLOCKS, STRIP, HALF), F32),
            pltpu.VMEM((OWNERS, 64, SIDE), F32),
            pltpu.VMEM((NY, 16, SIDE), F32),
            pltpu.VMEM((NX, 16, SIDE), F32),
            dma((BLOCKS + 4,)),
            dma((OWNERS,)),
            dma((OWNERS,)),
            dma((OWNERS,)),
            dma((OWNERS,)),
            dma((NX - 1, CHUNKS)),
            dma((NX - 1, CHUNKS)),
            dma((CHUNKS,)),
            dma((CHUNKS,)),
            dma((OWNERS,)),
            dma((OWNERS,)),
            dma((NY,)),
            dma((NY,)),
            dma((NX,)),
            dma((NX,)),
            dma((NY,)),
            dma((NY,)),
            dma((OWNERS,)),
            dma((OWNERS,)),
        ],
        compiler_params=pltpu.CompilerParams(
            collective_id=0, has_side_effects=True, vmem_limit_bytes=56 * 2**20
        ),
        name="step",
    )(packed, meta, object_field, probe, tables)


def on_device(object_field, probe, amplitude, tile_owner, row_start, col_start):
    tables = jnp.asarray(dft_tables())
    packed, meta = pack(tile_owner, row_start, col_start, amplitude)
    object_grad, probe_grad = step(packed, meta, object_field, probe, tables)
    return object_grad, probe_grad.reshape(2, SIDE, SIDE)


def solution(mesh):
    return jax.shard_map(
        on_device,
        mesh=mesh,
        in_specs=(
            P(None, None, "obj"),
            P(),
            P(("pat", "obj"), None, None),
            P(("pat", "obj"), None),
            P(("pat", "obj")),
            P(("pat", "obj")),
        ),
        out_specs=(P(None, "pat", "obj"), P()),
        check_vma=False,
    )
```

time: 842 us -> 122 us (0.14); the launches traced: 833 us -> 121 us
  waiting for transfers between devices: 302 us -> 0 us
  local copies, waits for them, and re-layouts: 212 us -> 5.48 us
  matrix products: 167 us -> 0 us
  Pallas kernels: 0 us -> 115 us
  loops' own time: 60.7 us -> 0 us
  other arithmetic: 52.1 us -> 0 us
  starting transfers between devices: 22.2 us -> 0 us
  between operations: 16.2 us -> 0.65 us
    all_to_all x4 -> x0, waiting for transfers between devices: 190 us -> none  [the longest x1 91.9 us: on_device(): lax.all_to_all(by_owner(local_res), 'obj', split_axis=0, concat_axis=0, t...]
    dot_general x18 -> x0, matrix products: 167 us -> none  [the longest x2 21.8 us: both_sides(): jnp.einsum('sjk,kl->sjl', left_re, table_im, precision=high)]
    pallas_call x0 -> x2, Pallas kernels: none -> 115 us  [the longest x1 111 us: step(): pl.pallas_call(step_kernel, out_shape=(jax.ShapeDtypeStruct((2, STRIP, TI...]
    reduce_scatter x1 -> x0, waiting for transfers between devices: 113 us -> none  [on_device(): lax.psum_scatter(gradient, 'pat', scatter_dimension=1, tiled=True)]
    dynamic_update_slice x16 -> x0, local copies, waits for them, and re-layouts: 101 us -> none  [add_window(): return lax.dynamic_update_slice(gradient, before + update[number], corner)]
    gather x48 -> x0, local copies, waits for them, and re-layouts: 64.9 us -> none
    another operation x2 -> x0, loops' own time: 60.7 us -> none  [the longest x1 60.6 us: on_device(): lax.fori_loop(0, slots, add_window, jnp.zeros(object_field.shape, jnp.flo...]
    add x16 -> x0, other arithmetic: 24.5 us -> none  [add_window(): return lax.dynamic_update_slice(gradient, before + update[number], corner)]
  transfers between devices with their start and end apart: 6 -> 0, of which waited for: 5 -> 0; matrix products, arithmetic and copies ran while one was open for 20% -> 0% of each run, Pallas kernels for 0% -> 0%
where the time goes in v2:
time: 122 us; the launch traced here: 121 us
  Pallas kernels  115 us (94%)
  local copies, waits for them, and re-layouts  5.48 us (4%)
    pallas_call x1, Pallas kernels, step(): pl.pallas_call(step_kernel, out_shape=(jax.ShapeDtypeStruct((2, STRIP, TI...  111 us
    unnamed x3, local copies, waits for them, and re-layouts  5.48 us
    pallas_call x1, Pallas kernels, pack(): pl.pallas_call(pack_kernel, out_shape=(jax.ShapeDtypeStruct((OWNERS, CAP,...  3.92 us

profile of v2, /device:TPU:1, one launch (start us, length us, event | category | flops | bytes accessed | tf_op | source)
XLA Modules:
  0.0 121.4 jit_solution(12254639141364605146)
XLA Ops:
  0.6 1.3 %copy.9.owner_ref = s32[8,1]{1,0:T(8,128)} copy(s32[8,1]{0,1:T(1,128)} %param.10) | data formatting | bytes 64 | tf_op args[3]
  2.0 3.9 %pack.1 = (f32[8,2,2,256,128]{4,3,2,1,0:T(8,128)}, s32[8,8,128]{2,1,0:T(8,128)}) custom-call(s32[8,1]{1,0:T(8,128)} %copy.9.owner_ref, s32[8]{0:T(128)} %row_ref.1, s32[8]{0:T(128)} %col_ref.1, f32[8,256,256]{2,1,0:T(8,128)} %amp_ref.1), custom_call_target="tpu_custom_call" | custom-call | tf_op jit(solution)/shard_map/pack/pallas_call | solution.py:183
  5.9 111.4 %step.1 = (f32[2,64,2048]{2,1,0:T(8,128)}, f32[512,256]{1,0:T(8,128)}) custom-call(f32[8,2,2,256,128]{4,3,2,1,0:T(8,128)} %get-tuple-element.6.packed_ref, s32[8,8,128]{2,1,0:T(8,128)} %get-tuple-element.7.meta_ref, f32[2,1024,2048]{2,1,0:T(8,128)} %object_ref.1, f32[2,256,256]{2,1,0:T(8,128)} %probe_ref.1, bf16[8,2,256,256]{3,2,1,0:T(8,128)(2,1)} %constant.2.clone.tables_ref), custom_call_target="tpu_custom_call" | custom-call | tf_op jit(solution)/shard_map/step/pallas_call | solution.py:520
  117.3 2.3 %copy.12 = f32[2,64,2048]{2,1,0:T(8,128)} copy(f32[2,64,2048]{2,1,0:T(8,128)} %get-tuple-element.12) | data formatting | bytes 2097152
  119.6 1.9 %copy.13 = f32[2,256,256]{2,1,0:T(8,128)} copy(f32[2,256,256]{2,1,0:T(8,128)} %bitcast.1) | data formatting | bytes 1048576

commit v3 on v2

--- a/solution.py
+++ b/solution.py
@@ -26,7 +26,7 @@
 CHUNK = BLOCKS // CHUNKS
 F32 = jnp.float32
 BF16 = jnp.bfloat16
-ANY = pl.BlockSpec(memory_space=pl.ANY)
+HBM = pl.BlockSpec(memory_space=pltpu.HBM)
 VMEM = pl.BlockSpec(memory_space=pltpu.VMEM)
 SMEM = pl.BlockSpec(memory_space=pltpu.SMEM)
 
@@ -160,13 +160,13 @@
     for j in range(COUNT):
         rank = jnp.int32(0)
         for i in range(j):
-            rank = rank + (owner_ref[i, 0] == owner_ref[j, 0]).astype(jnp.int32)
+            rank = rank + (owner_ref[0, i] == owner_ref[0, j]).astype(jnp.int32)
         ranks.append(rank)
     leaving = []
     for j in range(COUNT):
         for side in range(2):
             arriving(j, side).wait()
-        copy = pltpu.make_async_copy(held.at[j], packed_ref.at[owner_ref[j, 0], ranks[j]], leave.at[j])
+        copy = pltpu.make_async_copy(held.at[j], packed_ref.at[owner_ref[0, j], ranks[j]], leave.at[j])
         copy.start()
         leaving.append(copy)
     meta_ref[...] = jnp.zeros_like(meta_ref)
@@ -174,7 +174,7 @@
     for j in range(COUNT):
         mine = (sub // 4 == ranks[j]) & (sub % 4 < 3)
         value = jnp.where(sub % 4 == 0, 1, jnp.where(sub % 4 == 1, row_ref[j], col_ref[j]))
-        meta_ref[owner_ref[j, 0]] = jnp.where(mine, value, meta_ref[owner_ref[j, 0]])
+        meta_ref[owner_ref[0, j]] = jnp.where(mine, value, meta_ref[owner_ref[0, j]])
     for copy in leaving:
         copy.wait()
 
@@ -186,15 +186,15 @@
             jax.ShapeDtypeStruct((OWNERS, CAP, 2, SIDE, HALF), F32),
             jax.ShapeDtypeStruct((OWNERS, 8, 128), jnp.int32),
         ),
-        in_specs=[SMEM, SMEM, SMEM, ANY],
-        out_specs=(ANY, VMEM),
+        in_specs=[SMEM, SMEM, SMEM, HBM],
+        out_specs=(HBM, VMEM),
         scratch_shapes=[
             pltpu.VMEM((COUNT, 2, SIDE, HALF), F32),
             pltpu.SemaphoreType.DMA((COUNT, 2)),
             pltpu.SemaphoreType.DMA((COUNT,)),
         ],
         name="pack",
-    )(tile_owner, row_start, col_start, amplitude)
+    )(tile_owner.T, row_start, col_start, amplitude)
 
 
 def step_kernel(
@@ -248,31 +248,57 @@
     def metas(r):
         return remote(meta_ref.at[obj_at(r)], got_meta.at[r], send_meta.at[r], recv_meta.at[r], obj_peer(r))
 
-    def amplitudes(r):
-        return remote(packed_ref.at[obj_at(r)], got.at[r], send.at[r], recv.at[r], obj_peer(r))
+    def amplitudes(slot):
+        r = slot // CAP
+        n = lax.rem(slot, CAP)
+        return remote(
+            packed_ref.at[obj_at(r), n], got.at[r, n], send.at[slot], recv.at[slot], obj_peer(r)
+        )
+
+    stages = [
+        [2 * (2 * dz + side) + n for n in range(CAP) for dz in distances]
+        for side in (core, 1 - core)
+        for distances in ((1, 3), (2,))
+    ]
+
+    def start_stage(number):
+        for slot in stages[number]:
+            amplitudes(slot).start()
+
+    def end_stage(number):
+        for slot in stages[number]:
+            amplitudes(slot).wait_send()
 
     load_meta.start()
+    load_own.start()
+    for copy in loads:
+        copy.start()
     pl.semaphore_wait(barrier, len(peers))
     for r in range(1, OWNERS):
         metas(r).start()
-    amplitudes(1).start()
-    for dz in (1, 3, 2):
-        amplitudes(2 * dz + core).start()
-    load_own.start()
-    for copy in loads:
-        copy.start()
+    for slot in (2, 3):
+        amplitudes(slot).start()
+    start_stage(0)
     edge = jnp.zeros((2, STRIP, HALF), F32)
     for n in range(3 * SLOTS):
         pads[n, :, pl.ds(0, STRIP), :] = edge
         pads[n, :, pl.ds(STRIP + SIDE, STRIP), :] = edge
     pads[3 * SLOTS] = jnp.zeros((2, SPAN + STRIP, HALF), F32)
     part[...] = jnp.zeros_like(part)
-    load_meta.wait()
-    for r in range(1, OWNERS):
-        metas(r).wait_recv()
-    load_corners = pltpu.make_async_copy(got_meta, corners, load.at[BLOCKS + 3])
-    load_corners.start()
-    load_corners.wait()
+
+    def take_corners(pair):
+        if pair:
+            metas(2 * pair).wait_recv()
+            metas(2 * pair + 1).wait_recv()
+        else:
+            load_meta.wait()
+            metas(1).wait_recv()
+        rows = pl.ds(2 * pair, 2)
+        copy = pltpu.make_async_copy(got_meta.at[rows], corners.at[rows], load.at[BLOCKS + 3])
+        copy.start()
+        copy.wait()
+
+    take_corners(0)
     for copy in loads:
         copy.wait()
     load_own.wait()
@@ -296,21 +322,31 @@
         inner = lane < HALF - shift
         return beside(jnp.where(inner, turned[0], turned[1]), jnp.where(inner, turned[1], turned[2]))
 
-    def from_source(k, carry):
-        r = jnp.where(k < 4, k, jnp.where(k < 6, k + 2, k - 2))
-
-        @pl.when(k == jnp.where(core == 0, 6, 2))
-        def _():
-            for dz in (1, 3, 2):
-                amplitudes(2 * dz + core).wait_send()
-            for dz in (1, 3, 2):
-                amplitudes(2 * dz + 1 - core).start()
+    def from_pair(k, carry):
+        dz = jnp.where(k >= 6, 2, jnp.where(lax.rem(k, 2) == 0, 1, 3))
+        n = jnp.where(k >= 6, k - 6, (k - 2) // 2)
+        one = jnp.where(k < 2, 2 * k, 4 * dz + n)
+        two = jnp.where(k < 2, 2 * k + 1, 4 * dz + 2 + n)
+
+        for side, turn, number in ((0, 4, 0), (0, 7, 1), (1, 2, 0), (1, 2, 1), (1, 4, 2)):
+
+            @pl.when((core == side) & (k == turn))
+            def _():
+                end_stage(number)
+                start_stage(number + 1)
+
+        for pair, turn in ((1, 2), (3, 3), (2, 6)):
+
+            @pl.when(k == turn)
+            def _():
+                take_corners(pair)
 
         @pl.when(k > 0)
         def _():
-            amplitudes(r).wait_recv()
-
-        slots = [CAP * r + n for n in range(CAP)]
+            amplitudes(one).wait_recv()
+            amplitudes(two).wait_recv()
+
+        slots = [one, two]
         probe_re = probe_ref[0]
         probe_im = probe_ref[1]
         windows = [(window(slot, 0), window(slot, 1)) for slot in slots]
@@ -321,8 +357,8 @@
         def wanted_rows(j, parity):
             return by_parity(
                 beside(
-                    got[r, j, 0, pl.ds(parity, HALF, stride=2), :],
-                    got[r, j, 1, pl.ds(parity, HALF, stride=2), :],
+                    got[slots[j] // CAP, lax.rem(slots[j], CAP), 0, pl.ds(parity, HALF, stride=2), :],
+                    got[slots[j] // CAP, lax.rem(slots[j], CAP), 1, pl.ds(parity, HALF, stride=2), :],
                 )
             )
 
@@ -330,7 +366,7 @@
         part_re = part[pl.ds(0, SIDE), :]
         part_im = part[pl.ds(SIDE, SIDE), :]
         for j, slot in enumerate(slots):
-            keep = corners[r, 4 * j, 0] > 0
+            keep = corners[slot // CAP, 4 * lax.rem(slot, CAP), 0] > 0
             res_re = jnp.where(keep, residuals[j][0], 0.0)
             res_im = jnp.where(keep, residuals[j][1], 0.0)
             window_re, window_im = windows[j]
@@ -353,7 +389,7 @@
         part[pl.ds(SIDE, SIDE), :] = part_im
         return carry
 
-    lax.fori_loop(0, OWNERS, from_source, 0)
+    lax.fori_loop(0, OWNERS, from_pair, 0)
 
     def eighth(number):
         return pl.ds(pl.multiple_of(number * 64, 64), 64)
@@ -455,7 +491,19 @@
             along_x(c, k).start()
         return carry
 
-    lax.fori_loop(0, CHUNKS, gather_chunk, 0)
+    lax.fori_loop(0, CHUNKS // 2, gather_chunk, 0)
+
+    @pl.when(core == 1)
+    def _():
+        probe_step(0)
+        probe_step(1)
+
+    lax.fori_loop(CHUNKS // 2, CHUNKS, gather_chunk, 0)
+
+    @pl.when(core == 0)
+    def _():
+        end_stage(2)
+        start_stage(3)
 
     own_block = block(jnp.where(last, x + 1, 0))
     for c in range(CHUNKS):
@@ -476,11 +524,11 @@
         def _():
             along_y(c).start()
 
-        if c in (1, 3, 5, 6):
+        if c in (3, 4):
 
             @pl.when(core == 1)
             def _():
-                probe_step((1, 3, 5, 6).index(c))
+                probe_step(c - 1)
 
     for c in range(CHUNKS):
 
@@ -506,9 +554,9 @@
 
     for r in range(1, OWNERS):
         metas(r).wait_send()
-    amplitudes(1).wait_send()
-    for dz in (1, 3, 2):
-        amplitudes(2 * dz + 1 - core).wait_send()
+    for slot in (2, 3):
+        amplitudes(slot).wait_send()
+    end_stage(3)
     for c in range(CHUNKS):
         for k in range(1, NX):
             along_x(c, k).wait_send()
@@ -523,7 +571,7 @@
             jax.ShapeDtypeStruct((2, STRIP, TILE), F32),
             jax.ShapeDtypeStruct((2 * SIDE, SIDE), F32),
         ),
-        in_specs=[ANY, VMEM, ANY, VMEM, ANY],
+        in_specs=[HBM, VMEM, HBM, VMEM, HBM],
         out_specs=(VMEM, VMEM),
         scratch_shapes=[
             pltpu.VMEM((OWNERS, CAP, 2, SIDE, HALF), F32),
@@ -542,8 +590,8 @@
             pltpu.VMEM((NY, 16, SIDE), F32),
             pltpu.VMEM((NX, 16, SIDE), F32),
             dma((BLOCKS + 4,)),
-            dma((OWNERS,)),
-            dma((OWNERS,)),
+            dma((SLOTS,)),
+            dma((SLOTS,)),
             dma((OWNERS,)),
             dma((OWNERS,)),
             dma((NX - 1, CHUNKS)),
@@ -562,7 +610,7 @@
             dma((OWNERS,)),
         ],
         compiler_params=pltpu.CompilerParams(
-            collective_id=0, has_side_effects=True, vmem_limit_bytes=56 * 2**20
+            collective_id=0, has_side_effects=True, vmem_limit_bytes=48 * 2**20
         ),
         name="step",
     )(packed, meta, object_field, probe, tables)

time: 122 us -> 106 us (0.87)
  Pallas kernels: 115 us -> 100 us
    pallas_call x1, Pallas kernels: 111 us -> 96.3 us  [step(): pl.pallas_call(step_kernel, out_shape=(jax.ShapeDtypeStruct((2, STRIP, TI...]
    unnamed x3 -> x8, local copies, waits for them, and re-layouts: 5.48 us -> 5.15 us
where the time goes in v3:
time: 106 us
  Pallas kernels  100 us (94%)
  local copies, waits for them, and re-layouts  5.15 us (5%)
    pallas_call x1, Pallas kernels, step(): pl.pallas_call(step_kernel, out_shape=(jax.ShapeDtypeStruct((2, STRIP, TI...  96.3 us
    unnamed x8, local copies, waits for them, and re-layouts  5.15 us
    pallas_call x1, Pallas kernels, pack(): pl.pallas_call(pack_kernel, out_shape=(jax.ShapeDtypeStruct((OWNERS, CAP,...  3.87 us

profile of v3, /device:TPU:1, one launch (start us, length us, event | category | flops | bytes accessed | tf_op | source)
XLA Modules:
  0.0 106.0 jit_solution(6185702202703909867)
XLA Ops:
  0.6 3.9 %pack.1 = (f32[8,2,2,256,128]{4,3,2,1,0:T(8,128)}, s32[8,8,128]{2,1,0:T(8,128)}) custom-call(s32[1,8]{1,0:T(1,128)} %bitcast.3, s32[8]{0:T(128)} %row_ref.1, s32[8]{0:T(128)} %col_ref.1, f32[8,256,256]{2,1,0:T(8,128)} %amp_ref.1), custom_call_target="tpu_custom_call" | custom-call | tf_op jit(solution)/shard_map/pack/pallas_call | solution.py:183
  4.5 0.0 copy-start
  4.5 1.6 %copy-done = bf16[8,2,256,256]{3,2,1,0:T(8,128)(2,1)S(1)} copy-done((bf16[8,2,256,256]{3,2,1,0:T(8,128)(2,1)S(1)}, bf16[8,2,256,256]{3,2,1,0:T(8,128)(2,1)}, u32[]{:S(2)}) %copy-start) | copy-done | bytes 2097176
  6.1 0.0 copy-start.1
  6.1 1.0 copy-done.1
  7.1 0.0 copy-start.2
  7.1 0.8 copy-done.2
  7.9 96.3 %step.1 = (f32[2,64,2048]{2,1,0:T(8,128)S(1)}, f32[512,256]{1,0:T(8,128)S(1)}) custom-call(f32[8,2,2,256,128]{4,3,2,1,0:T(8,128)} %get-tuple-element.6.packed_ref, s32[8,8,128]{2,1,0:T(8,128)S(1)} %copy-done.2, f32[2,1024,2048]{2,1,0:T(8,128)} %object_ref.1, f32[2,256,256]{2,1,0:T(8,128)S(1)} %copy-done.1, bf16[8,2,256,256]{3,2,1,0:T(8,128)(2,1)S(1)} %copy-done), custom_call_target="tpu_custom_call" | custom-call | tf_op jit(solution)/shard_map/step/pallas_call | solution.py:568
  104.2 1.0 copy.11
  105.2 0.8 copy.12
Async XLA Ops:
  4.5 1.6 %copy-start = (bf16[8,2,256,256]{3,2,1,0:T(8,128)(2,1)S(1)}, bf16[8,2,256,256]{3,2,1,0:T(8,128)(2,1)}, u32[]{:S(2)}) copy-start(bf16[8,2,256,256]{3,2,1,0:T(8,128)(2,1)} %constant.2.clone.tables_ref) | copy-start | bytes 6291460
  6.1 1.0 copy-start.1
  7.1 0.8 copy-start.2

commit v4 on v3

--- a/solution.py
+++ b/solution.py
@@ -22,7 +22,7 @@
 SLOTS = OWNERS * CAP
 NX = 4
 NY = 4
-CHUNKS = 8
+CHUNKS = 16
 CHUNK = BLOCKS // CHUNKS
 F32 = jnp.float32
 BF16 = jnp.bfloat16
@@ -198,8 +198,8 @@
 
 
 def step_kernel(
-    packed_ref, meta_ref, object_ref, probe_ref, tables_ref, out_ref, total_ref,
-    got, got_meta, corners, strip, tables, pads, part, grad, got_x, got_y, own, rise, near, quarter, sixteenth,
+    packed_ref, meta_ref, object_ref, probe_hbm, tables_ref, out_ref, total_ref,
+    probe_ref, got, got_meta, corners, strip, tables, pads, part, grad, got_x, got_y, own, rise, near, quarter, sixteenth,
     load, send, recv, send_meta, recv_meta, send_x, recv_x, send_y, recv_y,
     send_a, recv_a, send_b, recv_b, send_c, recv_c, send_d, recv_d, send_e, recv_e,
 ):
@@ -242,6 +242,7 @@
         for n in range(BLOCKS)
     ]
     loads.append(pltpu.make_async_copy(tables_ref, tables, load.at[BLOCKS]))
+    loads.append(pltpu.make_async_copy(probe_hbm, probe_ref, load.at[BLOCKS + 4]))
     load_meta = pltpu.make_async_copy(meta_ref.at[me], got_meta.at[0], load.at[BLOCKS + 1])
     load_own = pltpu.make_async_copy(packed_ref.at[me], got.at[0], load.at[BLOCKS + 2])
 
@@ -328,12 +329,16 @@
         one = jnp.where(k < 2, 2 * k, 4 * dz + n)
         two = jnp.where(k < 2, 2 * k + 1, 4 * dz + 2 + n)
 
-        for side, turn, number in ((0, 4, 0), (0, 7, 1), (1, 2, 0), (1, 2, 1), (1, 4, 2)):
+        for side, turn, number in ((0, 4, 0), (1, 2, 0), (1, 2, 1), (1, 4, 2)):
 
             @pl.when((core == side) & (k == turn))
             def _():
                 end_stage(number)
                 start_stage(number + 1)
+
+        @pl.when((core == 0) & (k == 6))
+        def _():
+            start_stage(2)
 
         for pair, turn in ((1, 2), (3, 3), (2, 6)):
 
@@ -493,6 +498,12 @@
 
     lax.fori_loop(0, CHUNKS // 2, gather_chunk, 0)
 
+    @pl.when(core == 0)
+    def _():
+        end_stage(1)
+        end_stage(2)
+        start_stage(3)
+
     @pl.when(core == 1)
     def _():
         probe_step(0)
@@ -500,10 +511,6 @@
 
     lax.fori_loop(CHUNKS // 2, CHUNKS, gather_chunk, 0)
 
-    @pl.when(core == 0)
-    def _():
-        end_stage(2)
-        start_stage(3)
 
     own_block = block(jnp.where(last, x + 1, 0))
     for c in range(CHUNKS):
@@ -524,11 +531,11 @@
         def _():
             along_y(c).start()
 
-        if c in (3, 4):
+        if c in (6, 8):
 
             @pl.when(core == 1)
             def _():
-                probe_step(c - 1)
+                probe_step(c // 2 - 1)
 
     for c in range(CHUNKS):
 
@@ -571,9 +578,10 @@
             jax.ShapeDtypeStruct((2, STRIP, TILE), F32),
             jax.ShapeDtypeStruct((2 * SIDE, SIDE), F32),
         ),
-        in_specs=[HBM, VMEM, HBM, VMEM, HBM],
+        in_specs=[HBM, VMEM, HBM, HBM, HBM],
         out_specs=(VMEM, VMEM),
         scratch_shapes=[
+            pltpu.VMEM((2, SIDE, SIDE), F32),
             pltpu.VMEM((OWNERS, CAP, 2, SIDE, HALF), F32),
             pltpu.VMEM((OWNERS, 8, 128), jnp.int32),
             pltpu.SMEM((OWNERS, 8, 128), jnp.int32),
@@ -589,7 +597,7 @@
             pltpu.VMEM((OWNERS, 64, SIDE), F32),
             pltpu.VMEM((NY, 16, SIDE), F32),
             pltpu.VMEM((NX, 16, SIDE), F32),
-            dma((BLOCKS + 4,)),
+            dma((BLOCKS + 5,)),
             dma((SLOTS,)),
             dma((SLOTS,)),
             dma((OWNERS,)),

time: 106 us -> 105 us (level)
  no operation moved by 1% of the time
where the time goes in v4:
time: 105 us
  Pallas kernels  99.1 us (94%)
  local copies, waits for them, and re-layouts  5.15 us (5%)
    pallas_call x1, Pallas kernels, step(): pl.pallas_call(step_kernel, out_shape=(jax.ShapeDtypeStruct((2, STRIP, TI...  95.3 us
    unnamed x8, local copies, waits for them, and re-layouts  5.15 us
    pallas_call x1, Pallas kernels, pack(): pl.pallas_call(pack_kernel, out_shape=(jax.ShapeDtypeStruct((OWNERS, CAP,...  3.84 us

profile of v4, /device:TPU:1, one launch (start us, length us, event | category | flops | bytes accessed | tf_op | source)
XLA Modules:
  0.0 104.9 jit_solution(7505110532740460150)
XLA Ops:
  0.6 3.8 %pack.1 = (f32[8,2,2,256,128]{4,3,2,1,0:T(8,128)}, s32[8,8,128]{2,1,0:T(8,128)}) custom-call(s32[1,8]{1,0:T(1,128)} %bitcast.3, s32[8]{0:T(128)} %row_ref.1, s32[8]{0:T(128)} %col_ref.1, f32[8,256,256]{2,1,0:T(8,128)} %amp_ref.1), custom_call_target="tpu_custom_call" | custom-call | tf_op jit(solution)/shard_map/pack/pallas_call | solution.py:183
  4.5 0.0 copy-start
  4.5 1.6 %copy-done = bf16[8,2,256,256]{3,2,1,0:T(8,128)(2,1)S(1)} copy-done((bf16[8,2,256,256]{3,2,1,0:T(8,128)(2,1)S(1)}, bf16[8,2,256,256]{3,2,1,0:T(8,128)(2,1)}, u32[]{:S(2)}) %copy-start) | copy-done | bytes 2097176
  6.1 0.0 copy-start.1
  6.1 1.0 copy-done.1
  7.1 0.0 copy-start.2
  7.1 0.8 copy-done.2
  7.9 95.3 %step.1 = (f32[2,64,2048]{2,1,0:T(8,128)S(1)}, f32[512,256]{1,0:T(8,128)S(1)}) custom-call(f32[8,2,2,256,128]{4,3,2,1,0:T(8,128)} %get-tuple-element.6.packed_ref, s32[8,8,128]{2,1,0:T(8,128)S(1)} %copy-done.2, f32[2,1024,2048]{2,1,0:T(8,128)} %object_ref.1, f32[2,256,256]{2,1,0:T(8,128)S(1)} %copy-done.1, bf16[8,2,256,256]{3,2,1,0:T(8,128)(2,1)S(1)} %copy-done), custom_call_target="tpu_custom_call" | custom-call | tf_op jit(solution)/shard_map/step/pallas_call | solution.py:575
  103.2 1.0 copy.11
  104.2 0.8 copy.12
Async XLA Ops:
  4.5 1.6 %copy-start = (bf16[8,2,256,256]{3,2,1,0:T(8,128)(2,1)S(1)}, bf16[8,2,256,256]{3,2,1,0:T(8,128)(2,1)}, u32[]{:S(2)}) copy-start(bf16[8,2,256,256]{3,2,1,0:T(8,128)(2,1)} %constant.2.clone.tables_ref) | copy-start | bytes 6291460
  6.1 1.0 copy-start.1
  7.1 0.8 copy-start.2

commit v5 on v4

--- a/solution.py
+++ b/solution.py
@@ -578,7 +578,7 @@
             jax.ShapeDtypeStruct((2, STRIP, TILE), F32),
             jax.ShapeDtypeStruct((2 * SIDE, SIDE), F32),
         ),
-        in_specs=[HBM, VMEM, HBM, HBM, HBM],
+        in_specs=[HBM, HBM, HBM, HBM, HBM],
         out_specs=(VMEM, VMEM),
         scratch_shapes=[
             pltpu.VMEM((2, SIDE, SIDE), F32),
@@ -618,7 +618,7 @@
             dma((OWNERS,)),
         ],
         compiler_params=pltpu.CompilerParams(
-            collective_id=0, has_side_effects=True, vmem_limit_bytes=48 * 2**20
+            collective_id=0, has_side_effects=True, vmem_limit_bytes=51 * 2**20
         ),
         name="step",
     )(packed, meta, object_field, probe, tables)

time: 105 us -> 104 us (level)
  local copies, waits for them, and re-layouts: 5.15 us -> 3.56 us
    unnamed x8 -> x6, local copies, waits for them, and re-layouts: 5.15 us -> 3.56 us
where the time goes in v5:
time: 104 us; the launch traced here: 103 us
  Pallas kernels  99.1 us (95%)
  local copies, waits for them, and re-layouts  3.56 us (3%)
    pallas_call x1, Pallas kernels, step(): pl.pallas_call(step_kernel, out_shape=(jax.ShapeDtypeStruct((2, STRIP, TI...  95.2 us
    pallas_call x1, Pallas kernels, pack(): pl.pallas_call(pack_kernel, out_shape=(jax.ShapeDtypeStruct((OWNERS, CAP,...  3.85 us
    unnamed x6, local copies, waits for them, and re-layouts  3.56 us

profile of v5, /device:TPU:1, one launch (start us, length us, event | category | flops | bytes accessed | tf_op | source)
XLA Modules:
  0.0 103.3 jit_solution(6227196102518314175)
XLA Ops:
  0.6 3.8 %pack.1 = (f32[8,2,2,256,128]{4,3,2,1,0:T(8,128)}, s32[8,8,128]{2,1,0:T(8,128)}) custom-call(s32[1,8]{1,0:T(1,128)} %bitcast.3, s32[8]{0:T(128)} %row_ref.1, s32[8]{0:T(128)} %col_ref.1, f32[8,256,256]{2,1,0:T(8,128)} %amp_ref.1), custom_call_target="tpu_custom_call" | custom-call | tf_op jit(solution)/shard_map/pack/pallas_call | solution.py:183
  4.5 0.0 copy-start
  4.5 1.0 copy-done
  5.5 0.0 copy-start.1
  5.5 0.8 copy-done.1
  6.3 95.2 %step.1 = (f32[2,64,2048]{2,1,0:T(8,128)S(1)}, f32[512,256]{1,0:T(8,128)S(1)}) custom-call(f32[8,2,2,256,128]{4,3,2,1,0:T(8,128)} %get-tuple-element.6.packed_ref, s32[8,8,128]{2,1,0:T(8,128)S(1)} %copy-done.1, f32[2,1024,2048]{2,1,0:T(8,128)} %object_ref.1, f32[2,256,256]{2,1,0:T(8,128)S(1)} %copy-done, bf16[8,2,256,256]{3,2,1,0:T(8,128)(2,1)} %constant.2.clone.tables_ref), custom_call_target="tpu_custom_call" | custom-call | tf_op jit(solution)/shard_map/step/pallas_call | solution.py:575
  101.5 1.0 copy.11
  102.5 0.8 copy.12
Async XLA Ops:
  4.5 1.0 %copy-start = (f32[2,256,256]{2,1,0:T(8,128)S(1)}, f32[2,256,256]{2,1,0:T(8,128)}, u32[]{:S(2)}) copy-start(f32[2,256,256]{2,1,0:T(8,128)} %probe_hbm.1) | copy-start | bytes 1572868
  5.5 0.8 copy-start.1

commit v6 on v5

--- a/solution.py
+++ b/solution.py
@@ -271,15 +271,15 @@
             amplitudes(slot).wait_send()
 
     load_meta.start()
+    pl.semaphore_wait(barrier, len(peers))
+    for r in range(1, OWNERS):
+        metas(r).start()
+    start_stage(0)
+    for slot in (2, 3):
+        amplitudes(slot).start()
     load_own.start()
     for copy in loads:
         copy.start()
-    pl.semaphore_wait(barrier, len(peers))
-    for r in range(1, OWNERS):
-        metas(r).start()
-    for slot in (2, 3):
-        amplitudes(slot).start()
-    start_stage(0)
     edge = jnp.zeros((2, STRIP, HALF), F32)
     for n in range(3 * SLOTS):
         pads[n, :, pl.ds(0, STRIP), :] = edge
@@ -492,7 +492,7 @@
             return carry
 
         lax.fori_loop(c * CHUNK, (c + 1) * CHUNK, gather_block, 0)
-        for k in range(1, NX):
+        for k in (2, 1, 3):
             along_x(c, k).start()
         return carry
 

time: 104 us -> 102 us (0.981)
  Pallas kernels: 99.1 us -> 97.8 us
    pallas_call x1, Pallas kernels: 95.2 us -> 94 us  [step(): pl.pallas_call(step_kernel, out_shape=(jax.ShapeDtypeStruct((2, STRIP, TI...]
where the time goes in v6:
time: 102 us
  Pallas kernels  97.8 us (96%)
  local copies, waits for them, and re-layouts  3.56 us (3%)
    pallas_call x1, Pallas kernels, step(): pl.pallas_call(step_kernel, out_shape=(jax.ShapeDtypeStruct((2, STRIP, TI...  94 us
    pallas_call x1, Pallas kernels, pack(): pl.pallas_call(pack_kernel, out_shape=(jax.ShapeDtypeStruct((OWNERS, CAP,...  3.85 us
    unnamed x6, local copies, waits for them, and re-layouts  3.56 us

profile of v6, /device:TPU:1, one launch (start us, length us, event | category | flops | bytes accessed | tf_op | source)
XLA Modules:
  0.0 102.0 jit_solution(6433320565485779920)
XLA Ops:
  0.6 3.9 %pack.1 = (f32[8,2,2,256,128]{4,3,2,1,0:T(8,128)}, s32[8,8,128]{2,1,0:T(8,128)}) custom-call(s32[1,8]{1,0:T(1,128)} %bitcast.3, s32[8]{0:T(128)} %row_ref.1, s32[8]{0:T(128)} %col_ref.1, f32[8,256,256]{2,1,0:T(8,128)} %amp_ref.1), custom_call_target="tpu_custom_call" | custom-call | tf_op jit(solution)/shard_map/pack/pallas_call | solution.py:183
  4.5 0.0 copy-start
  4.5 1.0 %copy-done = f32[2,256,256]{2,1,0:T(8,128)S(1)} copy-done((f32[2,256,256]{2,1,0:T(8,128)S(1)}, f32[2,256,256]{2,1,0:T(8,128)}, u32[]{:S(2)}) %copy-start) | copy-done | bytes 524312
  5.5 0.0 copy-start.1
  5.5 0.8 copy-done.1
  6.3 94.0 %step.1 = (f32[2,64,2048]{2,1,0:T(8,128)S(1)}, f32[512,256]{1,0:T(8,128)S(1)}) custom-call(f32[8,2,2,256,128]{4,3,2,1,0:T(8,128)} %get-tuple-element.6.packed_ref, s32[8,8,128]{2,1,0:T(8,128)S(1)} %copy-done.1, f32[2,1024,2048]{2,1,0:T(8,128)} %object_ref.1, f32[2,256,256]{2,1,0:T(8,128)S(1)} %copy-done, bf16[8,2,256,256]{3,2,1,0:T(8,128)(2,1)} %constant.2.clone.tables_ref), custom_call_target="tpu_custom_call" | custom-call | tf_op jit(solution)/shard_map/step/pallas_call | solution.py:575
  100.3 1.0 copy.11
  101.2 0.8 copy.12
Async XLA Ops:
  4.5 1.0 %copy-start = (f32[2,256,256]{2,1,0:T(8,128)S(1)}, f32[2,256,256]{2,1,0:T(8,128)}, u32[]{:S(2)}) copy-start(f32[2,256,256]{2,1,0:T(8,128)} %probe_hbm.1) | copy-start | bytes 1572868
  5.5 0.8 copy-start.1

commit v7 on v6

--- a/solution.py
+++ b/solution.py
@@ -19,6 +19,7 @@
 SOFTEN = 0.25
 OWNERS = 8
 COUNT = 8
+SPARE = 4096
 SLOTS = OWNERS * CAP
 NX = 4
 NY = 4
@@ -147,58 +148,77 @@
     return residuals
 
 
-def pack_kernel(owner_ref, row_ref, col_ref, amp_ref, packed_ref, meta_ref, held, come, leave):
+def pack_kernel(
+    owner_ref, row_ref, col_ref, amp_ref, probe_ref, packed_ref, corners_ref, held, waves, meta_ref, come, leave
+):
     def arriving(j, side):
         return pltpu.make_async_copy(
             amp_ref.at[j, :, pl.ds(side * HALF, HALF)], held.at[j, side], come.at[j, side]
         )
 
+    def arriving_probe(part, side):
+        return pltpu.make_async_copy(
+            probe_ref.at[part, :, pl.ds(side * HALF, HALF)], waves.at[part, side], come.at[COUNT + part, side]
+        )
+
     for j in range(COUNT):
         for side in range(2):
             arriving(j, side).start()
+    for part in range(2):
+        for side in range(2):
+            arriving_probe(part, side).start()
     ranks = []
     for j in range(COUNT):
         rank = jnp.int32(0)
         for i in range(j):
             rank = rank + (owner_ref[0, i] == owner_ref[0, j]).astype(jnp.int32)
         ranks.append(rank)
-    leaving = []
+    meta_ref[...] = jnp.zeros_like(meta_ref)
+    sub = lax.broadcasted_iota(jnp.int32, (8, 128), 0)
+    for j in range(COUNT):
+        mine = (sub // 4 == ranks[j]) & (sub % 4 < 3)
+        value = jnp.where(sub % 4 == 0, 1, jnp.where(sub % 4 == 1, row_ref[j], col_ref[j]))
+        meta_ref[owner_ref[0, j]] = jnp.where(mine, value, meta_ref[owner_ref[0, j]])
+    leaving = [pltpu.make_async_copy(meta_ref, corners_ref.at[pl.ds(0, OWNERS)], leave.at[COUNT])]
+    leaving[0].start()
     for j in range(COUNT):
         for side in range(2):
             arriving(j, side).wait()
         copy = pltpu.make_async_copy(held.at[j], packed_ref.at[owner_ref[0, j], ranks[j]], leave.at[j])
         copy.start()
         leaving.append(copy)
-    meta_ref[...] = jnp.zeros_like(meta_ref)
-    sub = lax.broadcasted_iota(jnp.int32, (8, 128), 0)
-    for j in range(COUNT):
-        mine = (sub // 4 == ranks[j]) & (sub % 4 < 3)
-        value = jnp.where(sub % 4 == 0, 1, jnp.where(sub % 4 == 1, row_ref[j], col_ref[j]))
-        meta_ref[owner_ref[0, j]] = jnp.where(mine, value, meta_ref[owner_ref[0, j]])
+    for part in range(2):
+        for side in range(2):
+            arriving_probe(part, side).wait()
+    copy = pltpu.make_async_copy(waves, packed_ref.at[OWNERS], leave.at[COUNT + 1])
+    copy.start()
+    leaving.append(copy)
     for copy in leaving:
         copy.wait()
 
 
-def pack(tile_owner, row_start, col_start, amplitude):
+def pack(tile_owner, row_start, col_start, amplitude, probe):
     return pl.pallas_call(
         pack_kernel,
         out_shape=(
-            jax.ShapeDtypeStruct((OWNERS, CAP, 2, SIDE, HALF), F32),
-            jax.ShapeDtypeStruct((OWNERS, 8, 128), jnp.int32),
+            jax.ShapeDtypeStruct((OWNERS + 1, CAP, 2, SIDE, HALF), F32),
+            jax.ShapeDtypeStruct((SPARE, 8, 128), jnp.int32),
         ),
-        in_specs=[SMEM, SMEM, SMEM, HBM],
-        out_specs=(HBM, VMEM),
+        in_specs=[SMEM, SMEM, SMEM, HBM, HBM],
+        out_specs=(HBM, HBM),
         scratch_shapes=[
             pltpu.VMEM((COUNT, 2, SIDE, HALF), F32),
-            pltpu.SemaphoreType.DMA((COUNT, 2)),
-            pltpu.SemaphoreType.DMA((COUNT,)),
+            pltpu.VMEM((2, 2, SIDE, HALF), F32),
+            pltpu.VMEM((OWNERS, 8, 128), jnp.int32),
+            pltpu.SemaphoreType.DMA((COUNT + 2, 2)),
+            pltpu.SemaphoreType.DMA((COUNT + 2,)),
         ],
         name="pack",
-    )(tile_owner.T, row_start, col_start, amplitude)
+    )(tile_owner.T, row_start, col_start, amplitude, probe)
 
 
 def step_kernel(
-    packed_ref, meta_ref, object_ref, probe_hbm, tables_ref, out_ref, total_ref,
+    packed_ref, meta_ref, object_ref, tables_ref, out_ref, total_ref,
     probe_ref, got, got_meta, corners, strip, tables, pads, part, grad, got_x, got_y, own, rise, near, quarter, sixteenth,
     load, send, recv, send_meta, recv_meta, send_x, recv_x, send_y, recv_y,
     send_a, recv_a, send_b, recv_b, send_c, recv_c, send_d, recv_d, send_e, recv_e,
@@ -242,7 +262,7 @@
         for n in range(BLOCKS)
     ]
     loads.append(pltpu.make_async_copy(tables_ref, tables, load.at[BLOCKS]))
-    loads.append(pltpu.make_async_copy(probe_hbm, probe_ref, load.at[BLOCKS + 4]))
+    loads.append(pltpu.make_async_copy(packed_ref.at[OWNERS], probe_ref, load.at[BLOCKS + 4]))
     load_meta = pltpu.make_async_copy(meta_ref.at[me], got_meta.at[0], load.at[BLOCKS + 1])
     load_own = pltpu.make_async_copy(packed_ref.at[me], got.at[0], load.at[BLOCKS + 2])
 
@@ -352,8 +372,8 @@
             amplitudes(two).wait_recv()
 
         slots = [one, two]
-        probe_re = probe_ref[0]
-        probe_im = probe_ref[1]
+        probe_re = beside(probe_ref[0, 0], probe_ref[0, 1])
+        probe_im = beside(probe_ref[1, 0], probe_ref[1, 1])
         windows = [(window(slot, 0), window(slot, 1)) for slot in slots]
         exits = [
             (probe_re * re - probe_im * im, probe_re * im + probe_im * re) for re, im in windows
@@ -570,7 +590,7 @@
     probe_step(4)
 
 
-def step(packed, meta, object_field, probe, tables):
+def step(packed, meta, object_field, tables):
     dma = pltpu.SemaphoreType.DMA
     return pl.pallas_call(
         step_kernel,
@@ -578,10 +598,10 @@
             jax.ShapeDtypeStruct((2, STRIP, TILE), F32),
             jax.ShapeDtypeStruct((2 * SIDE, SIDE), F32),
         ),
-        in_specs=[HBM, HBM, HBM, HBM, HBM],
+        in_specs=[HBM, HBM, HBM, HBM],
         out_specs=(VMEM, VMEM),
         scratch_shapes=[
-            pltpu.VMEM((2, SIDE, SIDE), F32),
+            pltpu.VMEM((2, 2, SIDE, HALF), F32),
             pltpu.VMEM((OWNERS, CAP, 2, SIDE, HALF), F32),
             pltpu.VMEM((OWNERS, 8, 128), jnp.int32),
             pltpu.SMEM((OWNERS, 8, 128), jnp.int32),
@@ -621,13 +641,13 @@
             collective_id=0, has_side_effects=True, vmem_limit_bytes=51 * 2**20
         ),
         name="step",
-    )(packed, meta, object_field, probe, tables)
+    )(packed, meta, object_field, tables)
 
 
 def on_device(object_field, probe, amplitude, tile_owner, row_start, col_start):
     tables = jnp.asarray(dft_tables())
-    packed, meta = pack(tile_owner, row_start, col_start, amplitude)
-    object_grad, probe_grad = step(packed, meta, object_field, probe, tables)
+    packed, meta = pack(tile_owner, row_start, col_start, amplitude, probe)
+    object_grad, probe_grad = step(packed, meta, object_field, tables)
     return object_grad, probe_grad.reshape(2, SIDE, SIDE)
 
 

time: 102 us -> 99.9 us (0.979)
  local copies, waits for them, and re-layouts: 3.56 us -> 1.77 us
    unnamed x6 -> x2, local copies, waits for them, and re-layouts: 3.56 us -> 1.77 us
where the time goes in v7:
time: 99.9 us
  Pallas kernels  97.5 us (98%)
  local copies, waits for them, and re-layouts  1.77 us (2%)
    pallas_call x1, Pallas kernels, step(): pl.pallas_call(step_kernel, out_shape=(jax.ShapeDtypeStruct((2, STRIP, TI...  94 us
    pallas_call x1, Pallas kernels, pack(): pl.pallas_call(pack_kernel, out_shape=(jax.ShapeDtypeStruct((OWNERS + 1,...  3.5 us

profile of v7, /device:TPU:1, one launch (start us, length us, event | category | flops | bytes accessed | tf_op | source)
XLA Modules:
  0.0 99.9 jit_solution(16700859424145445591)
XLA Ops:
  0.6 3.5 %pack.1 = (f32[9,2,2,256,128]{4,3,2,1,0:T(8,128)}, s32[4096,8,128]{2,1,0:T(8,128)}) custom-call(s32[1,8]{1,0:T(1,128)} %bitcast.3, s32[8]{0:T(128)} %row_ref.1, s32[8]{0:T(128)} %col_ref.1, f32[8,256,256]{2,1,0:T(8,128)} %amp_ref.1, f32[2,256,256]{2,1,0:T(8,128)} %probe_ref.1), custom_call_target="tpu_custom_call" | custom-call | tf_op jit(solution)/shard_map/pack/pallas_call | solution.py:201
  4.1 94.0 %step.1 = (f32[2,64,2048]{2,1,0:T(8,128)S(1)}, f32[512,256]{1,0:T(8,128)S(1)}) custom-call(f32[9,2,2,256,128]{4,3,2,1,0:T(8,128)} %get-tuple-element.6.packed_ref, s32[4096,8,128]{2,1,0:T(8,128)} %get-tuple-element.7.meta_ref, f32[2,1024,2048]{2,1,0:T(8,128)} %object_ref.1, bf16[8,2,256,256]{3,2,1,0:T(8,128)(2,1)} %constant.2.clone.tables_ref), custom_call_target="tpu_custom_call" | custom-call | tf_op jit(solution)/shard_map/step/pallas_call | solution.py:595
  98.1 1.0 copy.11
  99.1 0.8 copy.12

commit v8 on v7

--- a/solution.py
+++ b/solution.py
@@ -356,7 +356,7 @@
                 end_stage(number)
                 start_stage(number + 1)
 
-        @pl.when((core == 0) & (k == 6))
+        @pl.when((core == 0) & (k == 5))
         def _():
             start_stage(2)
 

time: 99.9 us -> 100 us (level)
  no operation moved by 1% of the time
where the time goes in v8:
time: 100 us; the launch traced here: 99.9 us
  Pallas kernels  97.5 us (98%)
  local copies, waits for them, and re-layouts  1.77 us (2%)
    pallas_call x1, Pallas kernels, step(): pl.pallas_call(step_kernel, out_shape=(jax.ShapeDtypeStruct((2, STRIP, TI...  94 us
    pallas_call x1, Pallas kernels, pack(): pl.pallas_call(pack_kernel, out_shape=(jax.ShapeDtypeStruct((OWNERS + 1,...  3.5 us

profile of v8, /device:TPU:1, one launch (start us, length us, event | category | flops | bytes accessed | tf_op | source)
XLA Modules:
  0.0 99.9 jit_solution(12623387655278632875)
XLA Ops:
  0.6 3.5 %pack.1 = (f32[9,2,2,256,128]{4,3,2,1,0:T(8,128)}, s32[4096,8,128]{2,1,0:T(8,128)}) custom-call(s32[1,8]{1,0:T(1,128)} %bitcast.3, s32[8]{0:T(128)} %row_ref.1, s32[8]{0:T(128)} %col_ref.1, f32[8,256,256]{2,1,0:T(8,128)} %amp_ref.1, f32[2,256,256]{2,1,0:T(8,128)} %probe_ref.1), custom_call_target="tpu_custom_call" | custom-call | tf_op jit(solution)/shard_map/pack/pallas_call | solution.py:201
  4.1 94.0 %step.1 = (f32[2,64,2048]{2,1,0:T(8,128)S(1)}, f32[512,256]{1,0:T(8,128)S(1)}) custom-call(f32[9,2,2,256,128]{4,3,2,1,0:T(8,128)} %get-tuple-element.6.packed_ref, s32[4096,8,128]{2,1,0:T(8,128)} %get-tuple-element.7.meta_ref, f32[2,1024,2048]{2,1,0:T(8,128)} %object_ref.1, bf16[8,2,256,256]{3,2,1,0:T(8,128)(2,1)} %constant.2.clone.tables_ref), custom_call_target="tpu_custom_call" | custom-call | tf_op jit(solution)/shard_map/step/pallas_call | solution.py:595
  98.1 1.0 copy.11
  99.1 0.8 copy.12
